TPU v7x, 32 devices: a whole 2x2x4 slice. The times are simulated.
32 devices in a mesh: segment: 2 (over core), img: 16 (over z, y, x).
Axes of the slice: x: 2, y: 2, z: 4, core: 2. Of those that a mesh axis runs over, the one named last changes fastest.
Arguments:
- patch_tokens: bfloat16 [4, 128, 256, 384], P('segment', 'img'), may hold values from -6 to 6
- class_tokens: bfloat16 [4, 128, 384], P('segment', 'img'), may hold values from -6 to 6
- region_number: int32 [4, 128], P('segment'), may hold values from 0 to 2, as said below
- frozen_gain: bfloat16 [384], replicated, may hold values from 0.099609375 to 1.8984375
- frozen_triple: bfloat16 [384, 1152], replicated, may hold values from -0.3125 to 0.3125
- frozen_merge: bfloat16 [384, 384], replicated, may hold values from -1.25 to 1.25
- frozen_regain: bfloat16 [384], replicated, may hold values from 0.099609375 to 1.8984375
- frozen_expand: bfloat16 [384, 1536], replicated, may hold values from -0.3125 to 0.3125
- frozen_shrink: bfloat16 [1536, 384], replicated, may hold values from -0.15625 to 0.15625
- gain_first: bfloat16 [384], P('img'), may hold values from 0.099609375 to 1.8984375
- weight_triple: bfloat16 [384, 1152], P('img'), may hold values from -0.3125 to 0.3125
- weight_merge: bfloat16 [384, 384], P('img'), may hold values from -1.25 to 1.25
- gain_second: bfloat16 [384], P('img'), may hold values from 0.099609375 to 1.8984375
- weight_expand: bfloat16 [384, 1536], P('img'), may hold values from -0.3125 to 0.3125
- weight_shrink: bfloat16 [1536, 384], P('img'), may hold values from -0.15625 to 0.15625
- patch_cotangent: bfloat16 [4, 128, 256, 384], P('segment', 'img'), may hold values from -6 to 6
- region_cotangent: bfloat16 [4, 128, 384], P('segment', 'img'), may hold values from -6 to 6
Outputs:
- patch_output: bfloat16 [4, 128, 256, 384], P('segment', 'img')
- region_output: bfloat16 [4, 128, 384], P('segment', 'img')
- patch_gradient: bfloat16 [4, 128, 256, 384], P('segment', 'img')
- class_gradient: bfloat16 [4, 128, 384], P('segment', 'img')
- first_gradient: float32 [384], P('img')
- triple_gradient: float32 [384, 1152], P('img')
- merge_gradient: float32 [384, 384], P('img')
- second_gradient: float32 [384], P('img')
- expand_gradient: float32 [384, 1536], P('img')
- shrink_gradient: float32 [1536, 384], P('img')
Inputs may be any that keep to these rules, and one draw needn't show every extreme that they name: `region_number`: region numbers start at 0 and never fall along a micro-batch's 128 images; in each micro-batch one region begins among the first 8 images and ends among the last 8, with at most one region before it and one after it.
All inputs are finite; a program needn't handle non-finite values.
Results may differ from a plain program's by a relative error of at most 0.025.
Values may be sent and summed in bfloat16 or wider, within the bound.
A program may use at most 256 MiB of HBM per device.

v0:
```python
import jax
import jax.numpy as jnp
from jax import lax
from jax.sharding import PartitionSpec as P

HD = 64


epsilon = 1e-06


def partner(value, axis, bit):
    return lax.ppermute(value, axis, [(i, i ^ 1 << bit) for i in range(lax.axis_size(axis))])


def normalize(values, scaling):
    centred = values - jnp.mean(values, axis=-1, keepdims=True)
    inverse = lax.rsqrt(jnp.mean(centred * centred, axis=-1, keepdims=True) + epsilon)
    standard = centred * inverse
    return (standard * scaling, standard, inverse)


def normalize_back(upstream, standard, inverse, scaling):
    scaled = upstream * scaling
    centred = scaled - jnp.mean(scaled, axis=-1, keepdims=True)
    centred = centred - standard * jnp.mean(scaled * standard, axis=-1, keepdims=True)
    gain_grad = jnp.sum((upstream * standard).reshape(-1, upstream.shape[-1]), axis=0)
    return (centred * inverse, gain_grad)


def gelu_slope(hidden):
    return (
        0.5 * (1.0 + lax.erf(hidden * 0.7071067811865476))
        + hidden * jnp.exp(-0.5 * hidden * hidden) * 0.3989422804014327
    )


def forward_product(operand, weight):
    return lax.dot_general(
        operand, weight, (((operand.ndim - 1,), (0,)), ((), ())), preferred_element_type=jnp.float32
    )


def backward_product(upstream, weight):
    return lax.dot_general(
        upstream,
        weight,
        (((upstream.ndim - 1,), (1,)), ((), ())),
        preferred_element_type=jnp.float32,
    )


def row_product(operand, cotangent):
    left_rows = operand.reshape(-1, operand.shape[-1])
    right_rows = cotangent.reshape(-1, cotangent.shape[-1])
    return lax.dot_general(
        left_rows, right_rows, (((0,), (0,)), ((), ())), preferred_element_type=jnp.float32
    )


def heads_of(packed, portion):
    section_width = packed.shape[-1] // 3
    section = packed[..., portion * section_width : (portion + 1) * section_width]
    return section.reshape(packed.shape[:-1] + (section_width // HD, HD))


def raw_scores(queries, keyset, allowed):
    scores = jnp.einsum(
        "bqhd,bkhd->bhqk", queries, keyset, preferred_element_type=jnp.float32
    ) * HD ** (-0.5)
    if allowed is None:
        return scores
    return jnp.where(allowed[:, None], scores, -1e30)


def attend(queries, keyset, valueset, allowed):
    scores = raw_scores(queries, keyset, allowed)
    highest = jnp.max(scores, axis=-1, keepdims=True)
    logsum = highest + jnp.log(jnp.sum(jnp.exp(scores - highest), axis=-1, keepdims=True))
    weighting = jnp.exp(scores - logsum).astype(jnp.bfloat16)
    context = jnp.einsum("bhqk,bkhd->bqhd", weighting, valueset, preferred_element_type=jnp.float32)
    return (context.astype(jnp.bfloat16), logsum)


def score_terms(queries, keyset, valueset, allowed, logsum, context_grad):
    scores = raw_scores(queries, keyset, allowed)
    weighting = jnp.exp(scores - logsum)
    weight_grad = jnp.einsum(
        "bqhd,bkhd->bhqk", context_grad, valueset, preferred_element_type=jnp.float32
    )
    row_total = jnp.sum(weighting * weight_grad, axis=-1, keepdims=True)
    score_grad = (weighting * (weight_grad - row_total)).astype(jnp.bfloat16)
    return (weighting, score_grad, row_total)


def attend_back(queries, keyset, valueset, allowed, logsum, context_grad):
    weighting, score_grad, row_total = score_terms(
        queries, keyset, valueset, allowed, logsum, context_grad
    )
    value_grad = jnp.einsum(
        "bhqk,bqhd->bkhd",
        weighting.astype(jnp.bfloat16),
        context_grad,
        preferred_element_type=jnp.float32,
    )
    query_grad = jnp.einsum(
        "bhqk,bkhd->bqhd", score_grad, keyset, preferred_element_type=jnp.float32
    ) * HD ** (-0.5)
    key_grad = jnp.einsum(
        "bhqk,bqhd->bkhd", score_grad, queries, preferred_element_type=jnp.float32
    ) * HD ** (-0.5)
    return (query_grad, key_grad, value_grad)


def block_head(inputs, scaling, triple):
    normed, standard, inverse = normalize(inputs, scaling)
    first_low = normed.astype(jnp.bfloat16)
    packed = forward_product(first_low, triple).astype(jnp.bfloat16)
    return (first_low, standard, inverse, packed)


def block_tail(inputs, context, regain, merger, expand, shrink):
    middle = inputs + forward_product(context, merger)
    normed, standard, inverse = normalize(middle, regain)
    second = normed.astype(jnp.bfloat16)
    hidden = forward_product(second, expand)
    active = jax.nn.gelu(hidden, approximate=False).astype(jnp.bfloat16)
    result = middle + forward_product(active, shrink)
    return (result, (standard, inverse, second, hidden, active))


def tail_back(upstream, kept_tail, regain, merger, expand, shrink):
    standard, inverse, second, hidden, active = kept_tail
    out_low = upstream.astype(jnp.bfloat16)
    active_grad = backward_product(out_low, shrink)
    hidden_low = (active_grad * gelu_slope(hidden)).astype(jnp.bfloat16)
    second_grad = backward_product(hidden_low, expand)
    norm_grad, regain_grad = normalize_back(second_grad, standard, inverse, regain)
    middle_grad = upstream + norm_grad
    middle_low = middle_grad.astype(jnp.bfloat16)
    context_low = backward_product(middle_low, merger).astype(jnp.bfloat16)
    return (middle_grad, context_low, regain_grad, (middle_low, hidden_low, out_low))


def patch_forward(inputs, frozen):
    scaling, triple, merger, regain, expand, shrink = frozen
    first_low, standard, inverse, packed = block_head(inputs, scaling, triple)
    context, logsum = attend(heads_of(packed, 0), heads_of(packed, 1), heads_of(packed, 2), None)
    context = context.reshape(inputs.shape)
    result, kept_tail = block_tail(inputs, context, regain, merger, expand, shrink)
    return (result, (standard, inverse, packed, logsum, kept_tail))


def patch_backward(upstream, saved_state, frozen):
    scaling, triple, merger, regain, expand, shrink = frozen
    standard, inverse, packed, logsum, kept_tail = saved_state
    middle_grad, context_low, unused_gain, unused_rows = tail_back(
        upstream, kept_tail, regain, merger, expand, shrink
    )
    queries = heads_of(packed, 0)
    query_grad, key_grad, value_grad = attend_back(
        queries,
        heads_of(packed, 1),
        heads_of(packed, 2),
        None,
        logsum,
        context_low.reshape(queries.shape),
    )
    row_shape = upstream.shape
    packed_grad = jnp.concatenate(
        [query_grad.reshape(row_shape), key_grad.reshape(row_shape), value_grad.reshape(row_shape)],
        axis=-1,
    ).astype(jnp.bfloat16)
    norm_grad, unused_first = normalize_back(
        backward_product(packed_grad, triple), standard, inverse, scaling
    )
    return middle_grad + norm_grad


def local(
    patch_tokens,
    class_tokens,
    region_number,
    frozen_gain,
    frozen_triple,
    frozen_merge,
    frozen_regain,
    frozen_expand,
    frozen_shrink,
    gain_first,
    weight_triple,
    weight_merge,
    gain_second,
    weight_expand,
    weight_shrink,
    patch_cotangent,
    region_cotangent,
):
    micros, images, patches, model_width = patch_tokens.shape
    frozen = (
        frozen_gain.astype(jnp.float32),
        frozen_triple,
        frozen_merge,
        frozen_regain.astype(jnp.float32),
        frozen_expand,
        frozen_shrink,
    )
    joined = jnp.concatenate([class_tokens[:, :, None, :], patch_tokens], axis=2).astype(
        jnp.float32
    )
    joined = joined.reshape(micros * images, patches + 1, model_width)
    patch_result, saved_state = patch_forward(joined, frozen)
    patch_output = (
        patch_result[:, 1:, :].astype(jnp.bfloat16).reshape(micros, images, patches, model_width)
    )
    heads_sent = patch_result[:, 0, :].astype(jnp.bfloat16).reshape(micros, images, model_width)
    crossed = partner(heads_sent, "segment", 0)
    gathered = (
        lax.all_gather(gain_first, "img", axis=0, tiled=True),
        lax.all_gather(weight_triple, "img", axis=0, tiled=True),
        lax.all_gather(weight_merge, "img", axis=0, tiled=True),
        lax.all_gather(gain_second, "img", axis=0, tiled=True),
        lax.all_gather(weight_expand, "img", axis=0, tiled=True),
        lax.all_gather(weight_shrink, "img", axis=0, tiled=True),
    )
    full_gain, triple, merger, full_regain, expand, shrink = gathered
    scaling = full_gain.astype(jnp.float32)
    regain = full_regain.astype(jnp.float32)
    region_in = crossed.astype(jnp.float32)
    first_low, standard, inverse, packed = block_head(region_in, scaling, triple)
    local_keys = packed[..., model_width : 2 * model_width]
    local_values = packed[..., 2 * model_width :]
    all_keys, all_values = (
        lax.all_gather(local_keys, "img", axis=1, tiled=True),
        lax.all_gather(local_values, "img", axis=1, tiled=True),
    )
    head_shape = all_keys.shape[:-1] + (model_width // HD, HD)
    keyset = all_keys.reshape(head_shape)
    valueset = all_values.reshape(head_shape)
    queries = heads_of(packed, 0)
    first_slot = lax.axis_index("img") * images
    own_number = lax.dynamic_slice_in_dim(region_number, first_slot, images, 1)
    allowed = own_number[:, :, None] == region_number[:, None, :]
    context, logsum = attend(queries, keyset, valueset, allowed)
    context = context.reshape(region_in.shape)
    region_result, kept_tail = block_tail(region_in, context, regain, merger, expand, shrink)
    region_output = region_result.astype(jnp.bfloat16)
    upstream = region_cotangent.astype(jnp.float32)
    middle_grad, context_low, second_gain_grad, low_rows = tail_back(
        upstream, kept_tail, regain, merger, expand, shrink
    )
    middle_low, hidden_low, out_low = low_rows
    context_heads = context_low.reshape(queries.shape)
    query_grad, key_grad, value_grad = attend_back(
        queries, keyset, valueset, allowed, logsum, context_heads
    )
    key_sum, value_sum = (
        lax.psum_scatter(key_grad.reshape(all_keys.shape), "img", scatter_dimension=1, tiled=True),
        lax.psum_scatter(
            value_grad.reshape(all_values.shape), "img", scatter_dimension=1, tiled=True
        ),
    )
    packed_grad = jnp.concatenate(
        [query_grad.reshape(region_in.shape), key_sum, value_sum], axis=-1
    ).astype(jnp.bfloat16)
    norm_grad, first_gain_grad = normalize_back(
        backward_product(packed_grad, triple), standard, inverse, scaling
    )
    input_grad = (middle_grad + norm_grad).astype(jnp.bfloat16)
    returned = partner(input_grad, "segment", 0)
    patch_upstream = jnp.concatenate(
        [returned.astype(jnp.float32)[:, :, None, :], patch_cotangent.astype(jnp.float32)], axis=2
    )
    patch_input_grad = patch_backward(patch_upstream.reshape(joined.shape), saved_state, frozen)
    patch_gradient = (
        patch_input_grad[:, 1:, :]
        .astype(jnp.bfloat16)
        .reshape(micros, images, patches, model_width)
    )
    class_gradient = (
        patch_input_grad[:, 0, :].astype(jnp.bfloat16).reshape(micros, images, model_width)
    )
    second_low = kept_tail[2]
    active_low = kept_tail[4]
    shards = (
        lax.psum_scatter(first_gain_grad, "img", scatter_dimension=0, tiled=True),
        lax.psum_scatter(
            row_product(first_low, packed_grad), "img", scatter_dimension=0, tiled=True
        ),
        lax.psum_scatter(row_product(context, middle_low), "img", scatter_dimension=0, tiled=True),
        lax.psum_scatter(second_gain_grad, "img", scatter_dimension=0, tiled=True),
        lax.psum_scatter(
            row_product(second_low, hidden_low), "img", scatter_dimension=0, tiled=True
        ),
        lax.psum_scatter(row_product(active_low, out_low), "img", scatter_dimension=0, tiled=True),
    )
    totals = (
        lax.psum(shards[0].astype(jnp.bfloat16), "segment").astype(jnp.float32),
        lax.psum(shards[1].astype(jnp.bfloat16), "segment").astype(jnp.float32),
        lax.psum(shards[2].astype(jnp.bfloat16), "segment").astype(jnp.float32),
        lax.psum(shards[3].astype(jnp.bfloat16), "segment").astype(jnp.float32),
        lax.psum(shards[4].astype(jnp.bfloat16), "segment").astype(jnp.float32),
        lax.psum(shards[5].astype(jnp.bfloat16), "segment").astype(jnp.float32),
    )
    return (
        patch_output,
        region_output,
        patch_gradient,
        class_gradient,
        totals[0],
        totals[1],
        totals[2],
        totals[3],
        totals[4],
        totals[5],
    )


def solution(mesh):
    placed = (
        P("segment", "img", None, None),
        P("segment", "img", None),
        P("segment", None),
        P(),
        P(),
        P(),
        P(),
        P(),
        P(),
        P("img"),
        P("img", None),
        P("img", None),
        P("img"),
        P("img", None),
        P("img", None),
        P("segment", "img", None, None),
        P("segment", "img", None),
    )
    return jax.shard_map(
        local,
        mesh=mesh,
        in_specs=placed,
        out_specs=(
            P("segment", "img", None, None),
            P("segment", "img", None),
            P("segment", "img", None, None),
            P("segment", "img", None),
            P("img"),
            P("img", None),
            P("img", None),
            P("img"),
            P("img", None),
            P("img", None),
        ),
        check_vma=False,
    )
```

profile of v0, /device:TPU:0, one launch (start us, length us, event | category | flops | bytes accessed | tf_op | source)
XLA Modules:
  0.0 1223.5 jit_solution(2141186392069600719)
XLA Ops:
  16.3 7.4 convolution_convert_fusion
  27.6 6.2 copy.79
  46.2 18.5 %multiply_reduce_fusion.1 = (f32[16,6,257]{2,1,0:T(8,128)S(1)}, f32[16,6,257,257]{2,3,1,0:T(8,128)}) fusion(bf16[16,257,6,64]{1,3,2,0:T(8,128)(2,1)} %bitcast.143, bf16[16,257,6,64]{1,3,2,0:T(8,128)(2,1)} %bitcast.145), kind=kOutput, calls=%fused_computation.6 | convolution fusion | flops 824266880 | bytes 31777536 | tf_op jit(solution)/shard_map/bqhd,bkhd->bhqk/dot_general | solution.py:68
  64.7 16.7 %exponential_reduce_fusion = f32[16,6,257]{2,1,0:T(8,128)S(1)} fusion(f32[16,6,257,257]{2,3,1,0:T(8,128)} %get-tuple-element.43, f32[16,6,257]{2,1,0:T(8,128)S(1)} %get-tuple-element.42), kind=kLoop, calls=%fused_computation.5 | loop fusion | flops 18997440 | bytes 25560192 | tf_op jit(solution)/shard_map/reduce_sum | solution.py:79
  81.5 20.2 %convolution_convert_fusion.2 = bf16[16,6,64,257]{3,2,1,0:T(8,128)(2,1)} fusion(bf16[16,257,6,64]{1,3,2,0:T(8,128)(2,1)} %bitcast.149, f32[16,6,257,257]{2,3,1,0:T(8,128)} %get-tuple-element.43, f32[16,6,257]{2,1,0:T(8,128)S(1)} %log_add_fusion), kind=kOutput, calls=%fused_computation.88 | convolution fusion | flops 832211200 | bytes 31777536 | tf_op jit(solution)/shard_map/bhqk,bkhd->bqhd/dot_general | solution.py:81
  109.0 16.5 %fusion.17 = (u16[257,1536]{1,0:T(8,128)(2,1)S(1)}, u16[257,1536]{1,0:T(8,128)(2,1)S(1)}, f32[16,257,1536]{2,1,0:T(8,128)}) fusion(bf16[384,1536]{1,0:T(8,128)(2,1)S(1)} %copy-done, f32[16,257,384]{2,1,0:T(8,128)S(1)} %get-tuple-element.45, f32[384]{0:T(512)S(1)} %convert_element_type.157, f32[16,257]{1,0:T(8,128)S(1)} %add_rsqrt_fusion, ...), kind=kOutput, calls=%fused_computation.37 | convolution fusion | flops 4938347520 | bytes 34373248 | tf_op jit(solution)/shard_map/dot_general | solution.py:39
  125.6 65.5 %add_convert_fusion = bf16[16,257,384]{2,1,0:T(8,128)(2,1)S(1)} fusion(f32[16,257,384]{2,1,0:T(8,128)S(1)} %get-tuple-element.45, f32[16,257,1536]{2,1,0:T(8,128)} %get-tuple-element.46, u16[257,1536]{1,0:T(8,128)(2,1)S(1)} %get-tuple-element.11, u16[257,1536]{1,0:T(8,128)(2,1)S(1)} %get-tuple-element.10, bf16[1536,384]{1,0:T(8,128)(2,1)S(1)} %copy-done.35), kind=kOutput, calls=%fused_computation.67 | convolution fusion | flops 5295992832 | bytes 37496832 | tf_op jit(solution)/shard_map/dot_general | solution.py:39
  193.4 48.2 %all_gather.25 = bf16[384,1152]{1,0:T(8,128)(2,1)S(1)} all-gather(bf16[24,1152]{1,0:T(8,128)(2,1)S(1)} %copy-done.24), channel_id=1, replica_groups=mesh['segment'=2,'img'=16] {'img'}, dimensions={0}, use_global_device_ids=true | all-gather | bytes 940032 | tf_op jit(solution)/shard_map/all_gather | solution.py:220
  241.8 37.4 %all_gather.28 = bf16[384,384]{1,0:T(8,128)(2,1)S(1)} all-gather(bf16[24,384]{1,0:T(8,128)(2,1)S(1)} %copy-done.26), channel_id=1, replica_groups=mesh['segment'=2,'img'=16] {'img'}, dimensions={0}, use_global_device_ids=true | all-gather | bytes 313344 | tf_op jit(solution)/shard_map/all_gather | solution.py:221
  281.0 38.5 %all-reduce.7 = (bf16[384]{0:T(512)(128)(2,1)S(1)}, bf16[384]{0:T(512)(128)(2,1)S(1)}) all-reduce(bf16[384]{0:T(512)(128)(2,1)S(1)} %dynamic-update-slice, bf16[384]{0:T(512)(128)(2,1)S(1)} %dynamic-update-slice.1), channel_id=1, replica_groups=mesh['segment'=2,'img'=16] {'img'}, use_global_device_ids=true, to_apply=%add | all-reduce | flops 768 | bytes 3072
  320.1 36.6 %all_gather.26 = bf16[2,128,384]{2,1,0:T(8,128)(2,1)S(1)} all-gather(bf16[2,8,384]{2,1,0:T(8,128)(2,1)S(1)} %get-tuple-element.39), channel_id=1, replica_groups=mesh['segment'=2,'img'=16] {'img'}, dimensions={1}, use_global_device_ids=true | all-gather | bytes 208896 | tf_op jit(solution)/shard_map/all_gather | solution.py:235
  356.8 38.5 %all_gather.27 = bf16[2,128,384]{2,1,0:T(8,128)(2,1)S(1)} all-gather(bf16[2,8,384]{2,1,0:T(8,128)(2,1)S(1)} %get-tuple-element.38), channel_id=1, replica_groups=mesh['segment'=2,'img'=16] {'img'}, dimensions={1}, use_global_device_ids=true | all-gather | bytes 208896 | tf_op jit(solution)/shard_map/all_gather | solution.py:234
  407.6 114.3 %reduce-scatter.13.cloned.1.call-done = f32[2,8,384]{2,1,0:T(8,128)} async-done(((f32[2,128,384]{2,1,0:T(8,128)}), f32[2,8,384]{2,1,0:T(8,128)}) %reduce-scatter.13.cloned.1.call-update) | async-done | bytes 24592 | tf_op jit(solution)/shard_map/reduce_scatter | solution.py:259
  522.7 125.7 %reduce-scatter.11.cloned.1.call-done = f32[2,8,384]{2,1,0:T(8,128)} async-done(((f32[2,128,384]{2,1,0:T(8,128)}), f32[2,8,384]{2,1,0:T(8,128)}) %reduce-scatter.11.cloned.1.call-update) | async-done | bytes 24592 | tf_op jit(solution)/shard_map/reduce_scatter | solution.py:258
  663.8 40.0 %all-reduce.6 = (bf16[384]{0:T(512)(128)(2,1)S(1)}, bf16[384]{0:T(512)(128)(2,1)S(1)}) all-reduce(f32[384]{0:T(512)S(1)} %get-tuple-element.20, f32[384]{0:T(512)S(1)} %get-tuple-element.18), channel_id=4, replica_groups=mesh['segment'=2,'img'=16] {'img'}, use_global_device_ids=true, to_apply=%region_25.26.clone | all-reduce | flops 768 | bytes 4608
  705.0 20.0 %fusion.8.clone.1.clone.4 = bf16[16,257,1536]{2,1,0:T(8,128)(2,1)} fusion(f32[16,257,1536]{2,1,0:T(8,128)} %get-tuple-element.46, bf16[16,256,384]{2,1,0:T(8,128)(2,1)} %bitcast.163, bf16[16,1,384]{2,1,0:T(2,128)(2,1)S(1)} %copy.94, bf16[1536,384]{1,0:T(8,128)(2,1)} %param.25), kind=kOutput, calls=%fused_computation.15.clone.clone.clone.clone.clone.1 | convolution fusion | flops 4920188928 | bytes 42233856 | tf_op jit(solution)/shard_map/dot_general | solution.py:45
  725.1 10.7 multiply_reduce_fusion.5
  738.5 6.4 fusion.55
  751.2 18.7 %convolution_convert_fusion.1 = bf16[16,6,64,257]{3,2,1,0:T(8,128)(2,1)} fusion(bf16[16,257,6,64]{1,3,2,0:T(8,128)(2,1)} %bitcast.147, f32[16,6,257,257]{2,3,1,0:T(8,128)} %get-tuple-element.43, f32[16,6,257]{2,1,0:T(8,128)S(1)} %copy-done.5), kind=kOutput, calls=%fused_computation.87 | convolution fusion | flops 832211200 | bytes 31777536 | tf_op jit(solution)/shard_map/bhqk,bqhd->bkhd/dot_general | solution.py:100
  769.9 27.8 %multiply_reduce_fusion = (f32[16,6,257]{2,1,0:T(8,128)S(1)}, f32[16,6,257,257]{2,3,1,0:T(8,128)}) fusion(f32[16,6,257,257]{2,3,1,0:T(8,128)} %get-tuple-element.43, f32[16,6,257]{2,1,0:T(8,128)S(1)} %copy-done.5, bf16[16,257,6,64]{1,3,2,0:T(8,128)(2,1)} %bitcast.148, bf16[16,257,6,64]{1,3,2,0:T(8,128)(2,1)} %bitcast.150), kind=kOutput, calls=%fused_computation.1 | convolution fusion | flops 836948224 | bytes 57239040 | tf_op jit(solution)/shard_map/bqhd,bkhd->bhqk/dot_general | solution.py:88
  797.7 6.5 copy.101
  804.1 32.9 %multiply_convert_fusion = bf16[16,6,257,257]{2,3,1,0:T(8,128)(2,1)} fusion(f32[16,6,257,257]{2,3,1,0:T(8,128)} %get-tuple-element.58, f32[16,6,257,257]{2,3,1,0:T(8,128)} %get-tuple-element.43, f32[16,6,257]{2,1,0:T(8,128)S(1)} %get-tuple-element.57, f32[16,6,257]{2,1,0:T(8,128)S(1)} %copy-done.5), kind=kLoop, calls=%fused_computation | loop fusion | flops 31703520 | bytes 63604416 | tf_op jit(solution)/shard_map/convert_element_type | solution.py:92
  837.1 13.8 %multiply_convert_fusion.1 = bf16[16,6,64,257]{3,2,1,0:T(8,128)(2,1)} fusion(bf16[16,257,6,64]{1,3,2,0:T(8,128)(2,1)} %bitcast.144, bf16[16,6,257,257]{2,3,1,0:T(8,128)(2,1)} %multiply_convert_fusion), kind=kOutput, calls=%fused_computation.48 | convolution fusion | flops 814768128 | bytes 18997440 | tf_op jit(solution)/shard_map/bhqk,bqhd->bkhd/dot_general | solution.py:109
  850.8 6.3 copy.100
  857.2 14.6 %multiply_convert_fusion.2 = bf16[16,6,64,257]{3,2,1,0:T(8,128)(2,1)} fusion(bf16[16,257,6,64]{1,3,2,0:T(8,128)(2,1)} %bitcast.146, bf16[16,6,257,257]{2,3,1,0:T(8,128)(2,1)} %multiply_convert_fusion), kind=kOutput, calls=%fused_computation.49 | convolution fusion | flops 814768128 | bytes 18997440 | tf_op jit(solution)/shard_map/bhqk,bkhd->bqhd/dot_general | solution.py:106
  871.8 6.5 copy.99
  878.3 11.8 multiply_reduce_fusion.4
  891.5 13.7 %reduce-scatter.19.cloned.1.call-done = f32[24,1152]{1,0:T(8,128)} async-done(((f32[384,1152]{1,0:T(8,128)}), f32[24,1152]{1,0:T(8,128)}) %reduce-scatter.19.cloned.1.call-update) | async-done | bytes 110608
  906.9 131.3 %reduce-scatter.15.cloned.1.call-done = f32[24,1536]{1,0:T(8,128)} async-done(((f32[384,1536]{1,0:T(8,128)}), f32[24,1536]{1,0:T(8,128)}) %reduce-scatter.15.cloned.1.call-update) | async-done | bytes 147472 | tf_op jit(solution)/shard_map/reduce_scatter | solution.py:292
  1039.7 131.0 %reduce-scatter.17.cloned.1.call-done = f32[96,384]{1,0:T(8,128)} async-done(((f32[1536,384]{1,0:T(8,128)}), f32[96,384]{1,0:T(8,128)}) %reduce-scatter.17.cloned.1.call-update) | async-done | bytes 147472 | tf_op jit(solution)/shard_map/reduce_scatter | solution.py:295
  1172.3 10.4 fusion.37
  1196.1 17.1 %all-reduce.15.cloned.1.call-done = (bf16[24,1536]{1,0:T(8,128)(2,1)}, bf16[96,384]{1,0:T(8,128)(2,1)}) async-done(((bf16[24,1536]{1,0:T(8,128)(2,1)}, bf16[96,384]{1,0:T(8,128)(2,1)}), (bf16[24,1536]{1,0:T(8,128)(2,1)}, bf16[96,384]{1,0:T(8,128)(2,1)})) %all-reduce.15.cloned.1.call-update) | async-done | bytes 147472 | tf_op jit(solution)/shard_map/psum | solution.py:302
  (212 shorter events, 96.9 us)
Async XLA Ops:
  7.2 101.8 %copy-start = (bf16[384,1536]{1,0:T(8,128)(2,1)S(1)}, bf16[384,1536]{1,0:T(8,128)(2,1)}, u32[]{:S(2)}) copy-start(bf16[384,1536]{1,0:T(8,128)(2,1)} %param.24) | copy-start | bytes 3538948
  7.2 389.7 %all-gather.3.cloned.1.call-start = ((), (), s32[]{:S(2)}) async-start(), calls=%async_computation.6 | async-start | bytes 1253376 | tf_op jit(solution)/shard_map/all_gather | solution.py:223
  7.9 391.2 %all-gather.5.cloned.1.call-start = ((), (), s32[]{:S(2)}) async-start(), calls=%async_computation.7 | async-start | bytes 1253376 | tf_op jit(solution)/shard_map/all_gather | solution.py:224
  9.7 92.1 %copy-start.9 = (bf16[16,1,384]{2,1,0:T(2,128)(2,1)}, bf16[16,1,384]{2,1,0:T(2,128)(2,1)S(1)}, u32[]{:S(2)}) copy-start(bf16[16,1,384]{2,1,0:T(2,128)(2,1)S(1)} %copy.78) | copy-start | bytes 36868
  81.5 20.3 %copy-start.4 = (f32[16,6,257]{2,1,0:T(8,128)}, f32[16,6,257]{2,1,0:T(8,128)S(1)}, u32[]{:S(2)}) copy-start(f32[16,6,257]{2,1,0:T(8,128)S(1)} %log_add_fusion) | copy-start | bytes 296068
  81.5 27.5 %copy-start.30 = (f32[384]{0:T(512)}, f32[384]{0:T(512)S(1)}, u32[]{:S(2)}) copy-start(f32[384]{0:T(512)S(1)} %convert_element_type.157) | copy-start | bytes 4612
  81.5 20.3 %copy-start.2 = (bf16[2,8,256,384]{3,2,1,0:T(8,128)(2,1)S(1)}, bf16[2,8,256,384]{3,2,1,0:T(8,128)(2,1)}, u32[]{:S(2)}) copy-start(bf16[2,8,256,384]{3,2,1,0:T(8,128)(2,1)} %param.17) | copy-start | bytes 9437188
  81.5 20.3 %copy-start.38 = (bf16[384,384]{1,0:T(8,128)(2,1)S(1)}, bf16[384,384]{1,0:T(8,128)(2,1)}, u32[]{:S(2)}) copy-start(bf16[384,384]{1,0:T(8,128)(2,1)} %param.22) | copy-start | bytes 884740
  125.5 67.9 %copy-start.24 = (bf16[24,1152]{1,0:T(8,128)(2,1)S(1)}, bf16[24,1152]{1,0:T(8,128)(2,1)}, u32[]{:S(2)}) copy-start(bf16[24,1152]{1,0:T(8,128)(2,1)} %param.27) | copy-start | bytes 165892
  125.5 116.1 %copy-start.32 = (s32[2,128]{1,0:T(2,128)S(1)}, s32[2,128]{1,0:T(2,128)}, u32[]{:S(2)}) copy-start(s32[2,128]{1,0:T(2,128)} %param.19) | copy-start | bytes 3076
  125.5 116.3 %copy-start.26 = (bf16[24,384]{1,0:T(8,128)(2,1)S(1)}, bf16[24,384]{1,0:T(8,128)(2,1)}, u32[]{:S(2)}) copy-start(bf16[24,384]{1,0:T(8,128)(2,1)} %param.28) | copy-start | bytes 55300
  125.5 153.7 %copy-start.33 = (u32[32]{0:T(128)S(1)}, u32[32]{0:T(128)}, u32[]{:S(2)}) copy-start(u32[32]{0:T(128)} %constant.29) | copy-start | bytes 388
  125.5 154.9 %copy-start.40 = (bf16[24]{0:T(256)(128)(2,1)S(1)}, bf16[24]{0:T(256)(128)(2,1)}, u32[]{:S(2)}) copy-start(bf16[24]{0:T(256)(128)(2,1)} %param.26) | copy-start | bytes 148
  125.6 155.2 %copy-start.41 = (bf16[24]{0:T(256)(128)(2,1)S(1)}, bf16[24]{0:T(256)(128)(2,1)}, u32[]{:S(2)}) copy-start(bf16[24]{0:T(256)(128)(2,1)} %param.29) | copy-start | bytes 148
  125.6 273.5 %copy-start.25 = (bf16[2,8,384]{2,1,0:T(8,128)(2,1)S(1)}, bf16[2,8,384]{2,1,0:T(8,128)(2,1)}, u32[]{:S(2)}) copy-start(bf16[2,8,384]{2,1,0:T(8,128)(2,1)} %param.33) | copy-start | bytes 36868
  192.8 126.7 %collective-permute-start = (bf16[2,8,384]{2,1,0:T(8,128)(2,1)S(1)}, bf16[2,8,384]{2,1,0:T(8,128)(2,1)S(1)}, u32[]{:S(2)}, u32[]{:S(2)}) collective-permute-start(bf16[2,8,384]{2,1,0:T(8,128)(2,1)S(1)} %bitcast.175), channel_id=1, source_target_pairs={{0,16},{16,0},{1,17},{17,1},{2,18},{18,2},{3,19},{19,3},{4,20},{20... | collective-permute-start | bytes 36872 | tf_op jit(solution)/shard_map/ppermute | solution.py:13
  193.3 328.6 %reduce-scatter.13.cloned.1.call-start = ((), (), s32[]{:S(2)}) async-start(), calls=%async_computation.9 | async-start | bytes 417792 | tf_op jit(solution)/shard_map/reduce_scatter | solution.py:259
  399.1 259.4 %copy-start.11 = (f32[2,8,1536]{2,1,0:T(8,128)}, f32[2,8,1536]{2,1,0:T(8,128)S(1)}, u32[]{:S(2)}) copy-start(f32[2,8,1536]{2,1,0:T(8,128)S(1)} %get-tuple-element.51) | copy-start | bytes 294916
  404.3 244.1 %reduce-scatter.11.cloned.1.call-start = ((), (), s32[]{:S(2)}) async-start(), calls=%async_computation.8 | async-start | bytes 417792 | tf_op jit(solution)/shard_map/reduce_scatter | solution.py:258
  405.9 484.2 %reduce-scatter.21.cloned.1.call-start = ((), (), s32[]{:S(2)}) async-start(), calls=%async_computation.13 | async-start | bytes 626688
  407.2 498.0 %reduce-scatter.19.cloned.1.call-start = ((), (), s32[]{:S(2)}) async-start(), calls=%async_computation.12 | async-start | bytes 1880064
  650.9 387.2 %reduce-scatter.15.cloned.1.call-start = ((), (), s32[]{:S(2)}) async-start(), calls=%async_computation.10 | async-start | bytes 2506752 | tf_op jit(solution)/shard_map/reduce_scatter | solution.py:292
  653.0 517.7 %reduce-scatter.17.cloned.1.call-start = ((), (), s32[]{:S(2)}) async-start(), calls=%async_computation.11 | async-start | bytes 2506752 | tf_op jit(solution)/shard_map/reduce_scatter | solution.py:295
  660.6 530.4 %all-reduce.13.cloned.1.call-start = ((), (), s32[]{:S(2)}) async-start(), calls=%async_computation.14 | async-start | bytes 149504 | tf_op jit(solution)/shard_map/psum | solution.py:298
  661.2 43.8 %collective-permute-start.1 = (bf16[2,8,384]{2,1,0:T(8,128)(2,1)S(1)}, bf16[2,8,384]{2,1,0:T(8,128)(2,1)S(1)}, u32[]{:S(2)}, u32[]{:S(2)}) collective-permute-start(bf16[2,8,384]{2,1,0:T(8,128)(2,1)S(1)} %fusion.115), channel_id=1, source_target_pairs={{0,16},{16,0},{1,17},{17,1},{2,18},{18,2},{3,19},{19,3},{4,20},{20... | collective-permute-start | bytes 36872 | tf_op jit(solution)/shard_map/ppermute | solution.py:13
  661.3 63.8 %slice-start = ((s8[6488064]{0:T(1024)(128)(4,1)}), s8[2293760]{0:T(1024)(128)(4,1)S(1)}, s32[]{:S(2)}) async-start(s8[6488064]{0:T(1024)(128)(4,1)} %bitcast.159), calls=%async_computation.16 | async-start | bytes 4587520
  705.0 20.0 %slice-start.1 = ((s8[6488064]{0:T(1024)(128)(4,1)}), s8[4194304]{0:T(1024)(128)(4,1)S(1)}, s32[]{:S(2)}) async-start(s8[6488064]{0:T(1024)(128)(4,1)} %bitcast.159), calls=%async_computation.17 | async-start | bytes 8388608
  705.0 20.0 %copy-start.15 = (f32[16,257]{1,0:T(8,128)S(1)}, f32[16,257]{1,0:T(8,128)}, u32[]{:S(2)}) copy-start(f32[16,257]{1,0:T(8,128)} %copy-done.14) | copy-start | bytes 49348
  705.0 20.0 %copy-start.19 = (f32[16,257]{1,0:T(8,128)S(1)}, f32[16,257]{1,0:T(8,128)}, u32[]{:S(2)}) copy-start(f32[16,257]{1,0:T(8,128)} %copy-done.18) | copy-start | bytes 49348
  878.3 294.0 %copy-start.21 = (f32[16,257]{1,0:T(8,128)S(1)}, f32[16,257]{1,0:T(8,128)}, u32[]{:S(2)}) copy-start(f32[16,257]{1,0:T(8,128)} %copy-done.20) | copy-start | bytes 49348
  878.3 294.0 %copy-start.23 = (f32[16,257]{1,0:T(8,128)S(1)}, f32[16,257]{1,0:T(8,128)}, u32[]{:S(2)}) copy-start(f32[16,257]{1,0:T(8,128)} %copy-done.22) | copy-start | bytes 49348
  906.8 306.3 %all-reduce.15.cloned.1.call-start = ((), (), s32[]{:S(2)}) async-start(), calls=%async_computation.15 | async-start | bytes 294912 | tf_op jit(solution)/shard_map/psum | solution.py:302
  (24 other events, 240.0 us)
Sparse Core Ops, SparseCore 0:
  10.8 58.8 all-gather.2
  193.4 60.5 all-gather.4
  404.5 117.4 reduce-scatter.12
  527.7 120.6 reduce-scatter.10
  653.0 121.3 reduce-scatter.20
  779.8 125.3 reduce-scatter.18
  911.5 126.5 reduce-scatter.14
  1043.0 127.5 reduce-scatter.16
  1173.9 16.9 all-reduce.12
  1193.8 19.2 all-reduce.14
where the time goes:
time: 1230 us; the launch traced here: 1220 us
  waiting for transfers between devices  539 us (44%)
  matrix products  275 us (22%)
  blocking collectives  239 us (19%)
  other arithmetic  85.8 us (7%)
  local copies, waits for them, and re-layouts  66.9 us (5%)
  between operations  16.7 us (1%)
    reduce_scatter x1, waiting for transfers between devices, local(): lax.psum_scatter(row_product(second_low, hidden_low), 'img', scatter_dime...  131 us
    reduce_scatter x1, waiting for transfers between devices, local(): lax.psum_scatter(row_product(active_low, out_low), 'img', scatter_dimensi...  131 us
    reduce_scatter x1, waiting for transfers between devices, local(): lax.psum_scatter(key_grad.reshape(all_keys.shape), 'img', scatter_dimensi...  126 us
    reduce_scatter x1, waiting for transfers between devices, local(): lax.psum_scatter(value_grad.reshape(all_values.shape), 'img', scatter_dim...  114 us
    dot_general x8, matrix products, forward_product(): lax.dot_general(operand, weight, (((operand.ndim - 1,), (0,)), ((), ())),...  100 us
    unnamed x2, blocking collectives  78.6 us
    dot_general x8, matrix products, backward_product(): lax.dot_general(upstream, weight, (((upstream.ndim - 1,), (1,)), ((), ())...  53.1 us
    all_gather x1, blocking collectives, local(): lax.all_gather(weight_triple, 'img', axis=0, tiled=True)  48.2 us
  transfers between devices with their start and end apart: 12, of which 7 were waited for; matrix products, arithmetic and copies ran while one was open for 34% of the time, Pallas kernels for 0%

commit v1 on v0

v1 whole, which is shorter than its diff:
```python
import functools
from types import SimpleNamespace

import jax
import jax.numpy as jnp
from jax import lax
from jax.experimental import pallas as pl
from jax.experimental.pallas import tpu as pltpu
from jax.sharding import PartitionSpec as P

SEG = "segment"
IMG = "img"
HD = 64
HEADS8 = 8
EPSILON = 1e-06
LOG2E = 1.4426950408889634
LN2 = 0.6931471805599453
ROOT_HALF = 0.7071067811865476
DENSITY = 0.3989422804014327
F32 = jnp.float32
BF16 = jnp.bfloat16
MESH = pl.DeviceIdType.MESH
NEG = -1e30
PAD = 32

AT_FORWARD = 6
AT_REGION = 7


def nn(a, b):
    return lax.dot_general(a, b, (((1,), (0,)), ((), ())), preferred_element_type=F32)


def nt(a, b):
    return lax.dot_general(a, b, (((1,), (1,)), ((), ())), preferred_element_type=F32)


def tn(a, b):
    return lax.dot_general(a, b, (((0,), (0,)), ((), ())), preferred_element_type=F32)


def mean(values, axis):
    return jnp.sum(values, axis=axis, keepdims=True) * (1.0 / values.shape[axis])


def standardize(values, axis):
    centre = mean(values, axis)
    centred = values - centre
    inverse = lax.rsqrt(mean(centred * centred, axis) + EPSILON)
    return centred * inverse, centre, inverse


def norm_back(scaled, standard, inverse, axis):
    return inverse * (
        scaled - mean(scaled, axis) - standard * mean(scaled * standard, axis)
    )


def gelu_pair(hidden):
    upto = 0.5 + 0.5 * lax.erf(hidden * ROOT_HALF)
    bell = jnp.exp2(hidden * hidden * (-0.5 * LOG2E))
    return hidden * upto, upto + hidden * (bell * DENSITY)


def own_heads(rows, width):
    shape = (rows * HEADS8, width)
    lane = lax.broadcasted_iota(jnp.int32, shape, 1) // HD
    return lane == lax.rem(lax.broadcasted_iota(jnp.int32, shape, 0), HEADS8)


def spread(values):
    rows, width = values.shape
    tall = jnp.broadcast_to(values[:, None, :], (rows, HEADS8, width))
    return jnp.where(own_heads(rows, width), tall.reshape(rows * HEADS8, width), 0.0)


def gather_heads(values):
    tall, width = values.shape
    kept = jnp.where(own_heads(tall // HEADS8, width), values, 0.0)
    return jnp.sum(kept.reshape(tall // HEADS8, HEADS8, width), axis=1)


def wide_row(vectors, first, count):
    return jnp.concatenate([vectors[k : k + 1, :] for k in range(first, first + count)], axis=1)


def column(row, lanes):
    tall = jnp.broadcast_to(row, (128, row.shape[1])).T
    return jnp.concatenate([tall] * (lanes // 128), axis=1)


def pair_copy(source, target, sems, it):
    part = pl.ds(2 * it, 2)
    return pltpu.make_async_copy(source.at[part], target.at[part], sems.at[it])


def padded(values, shard, n):
    blank = jnp.zeros((PAD - shard, values.shape[1]), values.dtype)
    parts = []
    for j in range(n):
        parts += [values[shard * j : shard * (j + 1)], blank]
    return jnp.concatenate(parts, axis=0)


def trimmed(values, shard, n):
    return jnp.concatenate([values[PAD * j : PAD * j + shard] for j in range(n)], axis=0)


def patch_kernel(dims, *refs):
    r = SimpleNamespace(**dict(zip(dims.names, refs, strict=True)))
    n_img, width, hidden, inside = dims.n_img, dims.width, dims.hidden, dims.inside
    heads = width // HD
    rows, patches = dims.images, dims.patches
    pairs, lanes = rows // 2, 2 * patches
    shard = width // n_img
    shard_ff = hidden // n_img

    if inside:
        seg = lax.axis_index(SEG)
        me = lax.axis_index(IMG)
        barrier = pltpu.get_barrier_semaphore()

        def sibling(src, dst, link):
            return pltpu.make_async_remote_copy(
                src_ref=src,
                dst_ref=dst,
                send_sem=link.at[0],
                recv_sem=link.at[1],
                device_id={SEG: 1 - seg},
                device_id_type=MESH,
            )

        def to_peers(source, target, link):
            def send(step, carry):
                pltpu.make_async_remote_copy(
                    src_ref=source,
                    dst_ref=target,
                    send_sem=link.at[0],
                    recv_sem=link.at[1],
                    device_id={IMG: lax.rem(me + step, n_img)},
                    device_id_type=MESH,
                ).start()
                return carry

            lax.fori_loop(1, n_img, send, 0)
            pltpu.make_async_copy(source, target, link.at[1]).start()

        def to_other_segment(source, target, link):
            def send(step, carry):
                pltpu.make_async_remote_copy(
                    src_ref=source,
                    dst_ref=target,
                    send_sem=link.at[0],
                    recv_sem=link.at[1],
                    device_id={SEG: 1 - seg, IMG: lax.rem(me + step, n_img)},
                    device_id_type=MESH,
                ).start()
                return carry

            lax.fori_loop(0, n_img, send, 0)

        def wait_all(whole, sem):
            pltpu.make_async_copy(whole, whole, sem).wait()

        def greet(step, carry):
            peer = lax.rem(me + step, n_img)
            for other in range(2):
                pl.semaphore_signal(
                    barrier,
                    inc=1,
                    device_id={SEG: lax.rem(seg + other, 2), IMG: peer},
                    device_id_type=MESH,
                )
            return carry

        lax.fori_loop(1, n_img, greet, 0)
        pl.semaphore_signal(barrier, inc=1, device_id={SEG: 1 - seg}, device_id_type=MESH)

    for it in range(pairs):
        pair_copy(r.tokens, r.tok, r.tok_sem, it).start()
    for it in range(pairs):
        pair_copy(r.cotangent, r.cot, r.cot_sem, it).start()

    vectors = r.vectors[...]
    gain_row = wide_row(vectors, 0, width // 128)
    regain_row = wide_row(vectors, width // 128, width // 128)
    if inside:
        blank = jnp.zeros((PAD - shard, 4 * width), F32)
        triple = r.weight_triple[...].astype(F32)
        merge = r.weight_merge[...].astype(F32)
        expand = r.weight_expand[...].astype(F32)
        first_half = jnp.concatenate([triple, merge], axis=1)
        r.w_own[0] = jnp.concatenate([first_half, blank], axis=0).astype(BF16)
        r.w_own[1] = jnp.concatenate([expand, blank], axis=0).astype(BF16)
        for k in range(2):
            r.s_own[k] = r.weight_shrink[k * shard_ff // 2 : (k + 1) * shard_ff // 2, :]
            row = vectors[2 * width // 128 + k : 2 * width // 128 + k + 1, :]
            r.gain_own[k * shard : (k + 1) * shard, :] = column(row, 128)[0:shard]
        pl.semaphore_wait(barrier, 2 * n_img - 1)
        to_peers(r.gain_own, r.gains.at[me], r.l_gain)
        to_peers(r.region_cotangent, r.region_up.at[me], r.l_up)
        to_peers(r.w_own.at[seg], r.w_all.at[seg, me], r.l_weights)
        to_peers(r.s_own.at[seg], r.s_all.at[seg, me], r.l_shrink)

    r.tripleT[...] = r.frozen_triple[...].T
    r.mergeT[...] = r.frozen_merge[...].T
    r.expandT[...] = r.frozen_expand[...].T
    r.shrinkT[...] = r.frozen_shrink[...].T
    r.gainT[...] = column(gain_row, lanes)
    r.regainT[...] = column(regain_row, lanes)

    block_head = own_heads(1, width)
    class_in = r.class_tokens[...].astype(F32)
    class_unit, _, _ = standardize(class_in, 1)
    class_first = (class_unit * gain_row).astype(BF16)
    class_packed = nn(class_first, r.frozen_triple[...]).astype(BF16).astype(F32)
    r.class_packed[...] = class_packed
    tall_q = spread(class_packed[:, 0:width])
    tall_k = spread(class_packed[:, width : 2 * width])
    tall_v = spread(class_packed[:, 2 * width :])
    r.class_k[...] = tall_k.reshape(rows, HEADS8, width)
    r.class_v[...] = tall_v.reshape(rows, HEADS8, width)
    query_map = nt(tall_q.astype(BF16), r.frozen_triple[:, width : 2 * width])
    query_map = query_map * (LOG2E * HD ** (-0.5))
    r.query_map[...] = query_map.reshape(rows, HEADS8, width)
    self_score = jnp.sum(tall_q * tall_k, axis=1, keepdims=True) * (LOG2E * HD ** (-0.5))
    r.self_score[...] = jnp.broadcast_to(self_score, (rows * HEADS8, 128)).reshape(
        rows, HEADS8, 128
    )
    r.class_first[...] = jnp.broadcast_to(
        class_first.astype(F32)[:, None, :], (rows, HEADS8, width)
    )

    def class_forward(it, carry):
        pair_copy(r.tokens, r.tok, r.tok_sem, it).wait()
        values = jnp.concatenate([r.tok[2 * it + b].T for b in range(2)], axis=1).astype(F32)
        unit, centre, inverse = standardize(values, 0)
        first = (unit * r.gainT[...]).astype(BF16)
        r.firstT[it] = first
        r.stat[it, 0:1, :] = centre
        r.stat[it, 1:2, :] = inverse
        maps = jnp.concatenate([r.query_map[2 * it + b] for b in range(2)], axis=0)
        scores = nn(maps.astype(BF16), first)
        for b in range(2):
            part = scores[b * HEADS8 : (b + 1) * HEADS8, b * patches : (b + 1) * patches]
            alone = r.self_score[2 * it + b][:, 0:1]
            top = jnp.maximum(jnp.max(part, axis=1, keepdims=True), alone)
            weights = jnp.exp2(part - top)
            weight_alone = jnp.exp2(alone - top)
            share = 1.0 / (jnp.sum(weights, axis=1, keepdims=True) + weight_alone)
            weights = weights * share
            weight_alone = weight_alone * share
            r.class_probs[2 * it + b] = weights
            r.self_prob[2 * it + b] = jnp.broadcast_to(weight_alone, (HEADS8, 128))
            mixed = nt(weights.astype(BF16), first[:, b * patches : (b + 1) * patches])
            r.mixed[2 * it + b] = mixed + weight_alone * r.class_first[2 * it + b]
        return carry

    lax.fori_loop(0, pairs, class_forward, 0)

    mixed = r.mixed[...].reshape(rows * HEADS8, width).astype(BF16)
    class_context = gather_heads(nn(mixed, r.frozen_triple[:, 2 * width :])).astype(BF16)
    class_middle = class_in + nn(class_context, r.frozen_merge[...])
    class_unit_b, _, _ = standardize(class_middle, 1)
    class_second = (class_unit_b * regain_row).astype(BF16)
    class_active, class_slope = gelu_pair(nn(class_second, r.frozen_expand[...]))
    class_out = class_middle + nn(class_active.astype(BF16), r.frozen_shrink[...])
    r.class_context[...] = class_context.astype(F32)
    r.class_middle[...] = class_middle
    r.class_slope[...] = class_slope
    r.class_out[...] = class_out.astype(BF16)
    if inside:
        to_other_segment(r.class_out, r.crossed.at[me], r.l_crossed)

    def region():
        keys = n_img * rows
        wait_all(r.gains, r.l_gain.at[1])
        wait_all(r.region_up, r.l_up.at[1])
        wait_all(r.crossed, r.l_crossed.at[1])
        sibling(r.w_all.at[seg], r.w_all.at[seg], r.l_forward).wait()
        sibling(r.s_all.at[seg], r.s_all.at[seg], r.l_forward_shrink).wait()
        half = shard_ff // 2
        for j in range(n_img):
            for k in range(2):
                down = shard_ff * j + half * k
                r.region_shrink[down : down + half, :] = r.s_all[k, j]
        deep = PAD * n_img
        w_triple = r.w_all[0, :, :, 0 : 3 * width].reshape(deep, 3 * width)
        w_merge = r.w_all[0, :, :, 3 * width :].reshape(deep, width)
        w_expand = r.w_all[1].reshape(deep, hidden)
        wide = [r.gains[:, k * shard : (k + 1) * shard, :].reshape(width, 128) for k in range(2)]
        gain, regain = (jnp.concatenate([g] * (keys // 128), axis=1) for g in wide)

        slots = r.region_number.shape[1]
        per = slots // n_img
        micros = rows // per
        numbers = r.region_number[...].astype(F32)
        numbers = jnp.concatenate([numbers, jnp.zeros((8 - micros, slots), F32)], axis=0)
        at = lax.broadcasted_iota(jnp.int32, (slots, keys), 1)
        slot = lax.broadcasted_iota(jnp.int32, (slots, keys), 0)
        chosen = slot == per * (at // rows) + lax.rem(at, per)
        numbers = nn(numbers.astype(BF16), jnp.where(chosen, 1.0, 0.0).astype(BF16))
        at = lax.rem(lax.broadcasted_iota(jnp.int32, (1, keys), 1), rows) // per
        code = jnp.zeros((1, keys), F32)
        for m in range(micros):
            code = jnp.where(at == m, numbers[m : m + 1, :] * micros + m, code)
        code_down = jnp.broadcast_to(code, (128, keys)).T
        code_down = jnp.concatenate([code_down] * (keys // 128), axis=1)
        bias = jnp.where(code_down == code, 0.0, NEG)

        qkv, probs, ctx = r.qkv, r.probs, r.ctx
        values = r.crossed[...].reshape(keys, width).T.astype(F32)
        unit, _, inverse = standardize(values, 0)
        r.region_first[...] = padded(unit * gain, shard, n_img).astype(BF16)
        packed = tn(w_triple, r.region_first[...])
        qkv[0:width, 0:keys] = (packed[0:width] * (LOG2E * HD ** (-0.5))).astype(BF16)
        qkv[width:, 0:keys] = packed[width:].astype(BF16)
        mixes = []
        for h in range(heads):
            q = qkv[HD * h : HD * (h + 1), 0:keys]
            k = qkv[width + HD * h : width + HD * (h + 1), 0:keys]
            v = qkv[2 * width + HD * h : 2 * width + HD * (h + 1), 0:keys]
            scores = tn(k, q) + bias
            weights = jnp.exp2(scores - jnp.max(scores, axis=0, keepdims=True))
            share = 1.0 / jnp.sum(weights, axis=0, keepdims=True)
            low = weights.astype(BF16)
            probs[h] = low
            r.shares[0, h : h + 1, :] = share
            mixes.append(nn(v, low) * share)
        context = jnp.concatenate(mixes, axis=0)
        r.region_context[...] = padded(context, shard, n_img).astype(BF16)
        middle = values + tn(w_merge, r.region_context[...])
        unit_b, _, inverse_b = standardize(middle, 0)
        r.region_second[...] = padded(unit_b * regain, shard, n_img).astype(BF16)
        for c in range(0, hidden, width):
            at = slice(c, c + width)
            active, slope = gelu_pair(tn(w_expand[:, at], r.region_second[...]))
            r.region_active[at, :] = active.astype(BF16)
            r.slope[at, 0:keys] = slope.astype(BF16)
        result = middle + tn(r.region_shrink[...], r.region_active[...])
        mine = pl.ds(pl.multiple_of(me * rows, rows), rows)
        r.region_rows[...] = result.T
        r.region_out[...] = r.region_rows[mine, :].astype(BF16)

        upstream = r.region_up[...].reshape(keys, width).T
        for c in range(0, hidden, width):
            at = slice(c, c + width)
            active_grad = nn(r.region_shrink[at, :], upstream)
            r.active[at, 0:keys] = (active_grad * r.slope[at, 0:keys].astype(F32)).astype(BF16)
        hidden_low = r.active[:, 0:keys]
        second_grad = trimmed(nn(w_expand, hidden_low), shard, n_img)
        middle_grad = upstream.astype(F32) + norm_back(second_grad * regain, unit_b, inverse_b, 0)
        middle_low = middle_grad.astype(BF16)
        context_grad = trimmed(nn(w_merge, middle_low), shard, n_img)
        packed_grad = r.packed_grad
        for h in range(heads):
            at = slice(HD * h, HD * (h + 1))
            q = qkv[at, 0:keys]
            k = qkv[width + HD * h : width + HD * (h + 1), 0:keys]
            v = qkv[2 * width + HD * h : 2 * width + HD * (h + 1), 0:keys]
            part = context_grad[at] * r.shares[0, h : h + 1, :]
            total = jnp.sum(part * context[at], axis=0, keepdims=True)
            low = part.astype(BF16)
            weights = probs[h]
            score_grad = (weights.astype(F32) * (tn(v, low) - total)).astype(BF16)
            packed_grad[at, 0:keys] = (nn(k, score_grad) * HD ** (-0.5)).astype(BF16)
            packed_grad[width + HD * h : width + HD * (h + 1), 0:keys] = (
                nt(q, score_grad) * LN2
            ).astype(BF16)
            packed_grad[2 * width + HD * h : 2 * width + HD * (h + 1), 0:keys] = (
                nt(low, weights).astype(BF16)
            )
        first_grad = trimmed(nn(w_triple, packed_grad[:, 0:keys]), shard, n_img)
        back = norm_back(first_grad * gain, unit, inverse, 0)
        r.region_rows[...] = (middle_grad + back).T
        r.crossed_grad[...] = r.region_rows[mine, :].astype(BF16)
        sibling(r.crossed_grad, r.returned, r.l_returned).start()

        mine = pl.ds(pl.multiple_of(me * PAD, PAD), PAD)
        grads = r.grads
        grads[:, 0 : 3 * width] = nt(r.region_first[mine, :], packed_grad[:, 0:keys])[0:shard]
        grads[:, 3 * width : 4 * width] = nt(r.region_context[mine, :], middle_low)[0:shard]
        grads[:, 4 * width : 4 * width + hidden] = nt(r.region_second[mine, :], hidden_low)[0:shard]
        mine = pl.ds(pl.multiple_of(me * shard_ff, shard_ff), shard_ff)
        r.grads_shrink[...] = nt(r.region_active[mine, :], upstream)
        mine = pl.ds(pl.multiple_of(me * shard, shard), shard)
        for k, (grad, standard) in enumerate(((first_grad, unit), (second_grad, unit_b))):
            total = jnp.sum(grad * standard, axis=1, keepdims=True)
            r.gain_columns[...] = jnp.broadcast_to(total, (width, 128))
            at = 4 * width + hidden + 128 * k
            grads[:, at : at + 128] = r.gain_columns[mine, :]
        sibling(grads, r.grads_in, r.l_grads).start()
        sibling(r.grads_shrink, r.grads_shrink_in, r.l_grads_shrink).start()

    def patch_pair(it, carry):
        span = [slice(b * patches, (b + 1) * patches) for b in range(2)]
        qkv, ctx, probs = r.qkv, r.ctx, r.probs
        values = jnp.concatenate([r.tok[2 * it + b].T for b in range(2)], axis=1).astype(F32)
        first = r.firstT[it]
        queries = nn(r.tripleT[0:width, :], first) * (LOG2E * HD ** (-0.5))
        qkv[0:width, :] = queries.astype(BF16)
        qkv[width:, :] = nn(r.tripleT[width:, :], first).astype(BF16)
        for b in range(2):
            key_row = r.class_k[2 * it + b].astype(BF16)
            value_row = r.class_v[2 * it + b].astype(BF16)
            class_scores = nn(key_row, qkv[0:width, span[b]])
            mixes, class_weights, shares = [], [], []
            for h in range(heads):
                q = qkv[HD * h : HD * (h + 1), span[b]]
                k = qkv[width + HD * h : width + HD * (h + 1), span[b]]
                v = qkv[2 * width + HD * h : 2 * width + HD * (h + 1), span[b]]
                scores = tn(k, q)
                class_score = class_scores[h : h + 1, :]
                top = jnp.maximum(jnp.max(scores, axis=0, keepdims=True), class_score)
                weights = jnp.exp2(scores - top)
                class_weight = jnp.exp2(class_score - top)
                share = 1.0 / (jnp.sum(weights, axis=0, keepdims=True) + class_weight)
                low = weights.astype(BF16)
                probs[b * heads + h] = low
                mixes.append(nn(v, low))
                class_weights.append(class_weight)
                shares.append(share)
            blank = [jnp.zeros((HEADS8 - heads, patches), F32)]
            class_weights = jnp.concatenate(class_weights + blank, axis=0)
            r.class_weights[b] = class_weights
            r.shares[b] = jnp.concatenate(shares + blank, axis=0)
            from_class = tn(value_row, class_weights.astype(BF16))
            for h in range(heads):
                at = slice(HD * h, HD * (h + 1))
                ctx[at, span[b]] = ((mixes[h] + from_class[at]) * shares[h]).astype(BF16)
        middle = values + nn(r.mergeT[...], ctx[...])
        unit_b, _, inverse_b = standardize(middle, 0)
        second = (unit_b * r.regainT[...]).astype(BF16)
        chunk = width
        for c in range(0, hidden, chunk):
            at = slice(c, c + chunk)
            active, slope = gelu_pair(nn(r.expandT[at, :], second))
            r.active[at, :] = active.astype(BF16)
            r.slope[at, :] = slope.astype(BF16)
        result = middle + nn(r.shrinkT[...], r.active[...])
        for b in range(2):
            r.tok[2 * it + b] = result[:, span[b]].astype(BF16).T
        pair_copy(r.tok, r.patch_rows, r.out_sem, it).start()
        pair_copy(r.cotangent, r.cot, r.cot_sem, it).wait()
        upstream = jnp.concatenate([r.cot[2 * it + b].T for b in range(2)], axis=1)
        for c in range(0, hidden, chunk):
            at = slice(c, c + chunk)
            active_grad = nn(r.frozen_shrink[at, :], upstream)
            r.active[at, :] = active_grad.astype(BF16) * r.slope[at, :]
        second_grad = nn(r.frozen_expand[...], r.active[...])
        middle_grad = upstream.astype(F32) + norm_back(
            second_grad * r.regainT[...], unit_b, inverse_b, 0
        )
        context_grad = nn(r.frozen_merge[...], middle_grad.astype(BF16))
        low_grad, packed_grad = r.low_grad, r.packed_grad
        for b in range(2):
            key_row = r.class_k[2 * it + b].astype(BF16)
            value_row = r.class_v[2 * it + b].astype(BF16)
            totals = []
            for h in range(heads):
                at = slice(HD * h, HD * (h + 1))
                part = context_grad[at, span[b]] * r.shares[b][h : h + 1, :]
                totals.append(
                    jnp.sum(part * ctx[at, span[b]].astype(F32), axis=0, keepdims=True)
                )
                low_grad[at, span[b]] = part.astype(BF16)
            blank = [jnp.zeros((HEADS8 - heads, patches), F32)]
            all_low = low_grad[:, span[b]]
            class_weights = r.class_weights[b]
            class_grad = class_weights * (
                nn(value_row, all_low) - jnp.concatenate(totals + blank, axis=0)
            )
            class_grad = class_grad.astype(BF16)
            from_class = tn(key_row, class_grad)
            dk = nt(class_grad, qkv[0:width, span[b]]) * LN2
            dv = nt(class_weights.astype(BF16), all_low)
            r.class_dk[2 * it + b] = jnp.where(block_head, dk, 0.0)
            r.class_dv[2 * it + b] = jnp.where(block_head, dv, 0.0)
            for h in range(heads):
                at = slice(HD * h, HD * (h + 1))
                q = qkv[at, span[b]]
                k = qkv[width + HD * h : width + HD * (h + 1), span[b]]
                v = qkv[2 * width + HD * h : 2 * width + HD * (h + 1), span[b]]
                low = low_grad[at, span[b]]
                weights = probs[b * heads + h]
                score_grad = weights * (tn(v, low) - totals[h]).astype(BF16)
                value_grad = nt(low, weights)
                key_grad = nt(q, score_grad) * LN2
                query_grad = (nn(k, score_grad) + from_class[at]) * HD ** (-0.5)
                packed_grad[at, span[b]] = query_grad.astype(BF16)
                packed_grad[width + HD * h : width + HD * (h + 1), span[b]] = key_grad.astype(BF16)
                packed_grad[2 * width + HD * h : 2 * width + HD * (h + 1), span[b]] = (
                    value_grad.astype(BF16)
                )
        first_grad = nn(r.frozen_triple[...], packed_grad[...])
        centre, inverse = r.stat[it, 0:1, :], r.stat[it, 1:2, :]
        unit = (values - centre) * inverse
        back = norm_back(first_grad * r.gainT[...], unit, inverse, 0)
        r.input_grad[it] = (middle_grad + back).astype(BF16)

        pltpu.make_async_copy(r.input_grad.at[it], r.grad_rows.at[it], r.grad_sem.at[it]).start()

        if inside:

            @pl.when(it == AT_FORWARD)
            def _():
                wait_all(r.w_all.at[seg], r.l_weights.at[1])
                wait_all(r.s_all.at[seg], r.l_shrink.at[1])
                sibling(r.w_all.at[seg], r.w_all.at[seg], r.l_forward).start()
                sibling(r.s_all.at[seg], r.s_all.at[seg], r.l_forward_shrink).start()

            pl.when(it == AT_REGION)(region)
        return carry

    for it in range(pairs):
        pltpu.make_async_copy(r.firstT.at[it], r.first_rows.at[it], r.first_sem.at[it]).start()
    lax.fori_loop(0, pairs, patch_pair, 0)

    r.class_grads[:, 0:width] = jnp.sum(r.class_dk[...], axis=1)
    r.class_grads[:, width:] = jnp.sum(r.class_dv[...], axis=1)
    if inside:
        sibling(r.crossed_grad, r.returned, r.l_returned).wait()
        sibling(r.grads, r.grads_in, r.l_grads).wait()
        sibling(r.grads_shrink, r.grads_shrink_in, r.l_grads_shrink).wait()
        r.class_up[...] = r.returned[...]
        r.grads_out[...] = r.grads[...] + r.grads_in[...]
        r.shrink_out[...] = r.grads_shrink[...] + r.grads_shrink_in[...]
        peers = pl.ds(0, n_img - 1)
        wait_all(r.gains.at[peers], r.l_gain.at[0])
        wait_all(r.region_up.at[peers], r.l_up.at[0])
        wait_all(r.w_all.at[0, peers], r.l_weights.at[0])
        wait_all(r.s_all.at[0, peers], r.l_shrink.at[0])
        wait_all(r.crossed, r.l_crossed.at[0])
    for it in range(pairs):
        pair_copy(r.tok, r.patch_rows, r.out_sem, it).wait()
        pltpu.make_async_copy(r.firstT.at[it], r.first_rows.at[it], r.first_sem.at[it]).wait()
        pltpu.make_async_copy(r.input_grad.at[it], r.grad_rows.at[it], r.grad_sem.at[it]).wait()


def class_kernel(dims, *refs):
    r = SimpleNamespace(**dict(zip(dims.names, refs, strict=True)))
    width = dims.width
    rows, patches = dims.images, dims.patches
    pairs, lanes = rows // 2, 2 * patches
    it = pl.program_id(0)
    gain_row = wide_row(r.vectors[...], 0, width // 128)
    regain_row = wide_row(r.vectors[...], width // 128, width // 128)

    @pl.when(it == 0)
    def _():
        r.gainT[...] = column(gain_row, lanes)
        r.ungainT[...] = 1.0 / r.gainT[...]
        upstream = r.class_up[...]
        middle = r.class_middle[...]
        unit, _, inverse = standardize(middle, 1)
        hidden_low = (nt(upstream, r.frozen_shrink[...]) * r.class_slope[...]).astype(BF16)
        second_grad = nt(hidden_low, r.frozen_expand[...])
        middle_grad = upstream.astype(F32) + norm_back(second_grad * regain_row, unit, inverse, 1)
        r.middle_grad[...] = middle_grad
        low = nt(middle_grad.astype(BF16), r.frozen_merge[...]).astype(BF16).astype(F32)
        r.class_low[...] = low
        low_map = nt(spread(low).astype(BF16), r.frozen_triple[:, 2 * width :])
        r.low_map[...] = low_map.reshape(rows, HEADS8, width)
        total = jnp.sum(spread(low * r.class_context[...]), axis=1, keepdims=True)
        r.class_total[...] = jnp.broadcast_to(total, (rows * HEADS8, 128)).reshape(
            rows, HEADS8, 128
        )

    first = r.first_rows[0]
    maps = jnp.concatenate([r.low_map[2 * it + b] for b in range(2)], axis=0)
    probs_grads = nn(maps.astype(BF16), first)
    corrections = []
    for b in range(2):
        image = 2 * it + b
        own_first = first[:, b * patches : (b + 1) * patches]
        part = probs_grads[b * HEADS8 : (b + 1) * HEADS8, b * patches : (b + 1) * patches]
        weights = r.class_probs[b]
        score_grad = weights * (part - r.class_total[image][:, 0:1])
        r.mixed[image] = nt(score_grad.astype(BF16), own_first)
        left = jnp.concatenate([r.query_map[b], r.low_map[image]], axis=0)
        right = jnp.concatenate([score_grad * LN2, weights], axis=0)
        corrections.append(tn(left.astype(BF16), right.astype(BF16)))
    correction = jnp.concatenate(corrections, axis=1)
    inverse = r.stat[0, 1:2, :]
    scaled = correction * r.gainT[...]
    firsts = first.astype(F32)
    along = mean(correction * firsts, 0)
    back = inverse * (scaled - mean(scaled, 0) - firsts * r.ungainT[...] * along)
    result = r.grad_rows[0].astype(F32) + back
    for b in range(2):
        r.patch_gradient[b] = result[:, b * patches : (b + 1) * patches].astype(BF16).T
    r.patch_output[...] = r.patch_rows[...]

    @pl.when(it == pairs - 1)
    def _():
        low = r.class_low[...]
        packed = r.class_packed[...]
        tall_low = spread(low)
        total = r.class_total[...].reshape(rows * HEADS8, 128)[:, 0:1]
        self_prob = r.self_prob[...].reshape(rows * HEADS8, 128)[:, 0:1]
        tall_q = spread(packed[:, 0:width])
        tall_v = spread(packed[:, 2 * width :])
        self_grad = self_prob * (jnp.sum(tall_low * tall_v, axis=1, keepdims=True) - total)
        unit, _, inverse = standardize(r.class_tokens[...].astype(F32), 1)
        first = (unit * gain_row).astype(BF16).astype(F32)
        firsts = jnp.broadcast_to(first[:, None, :], (rows, HEADS8, width))
        mixed = r.mixed[...].reshape(rows * HEADS8, width)
        mixed = mixed + self_grad * firsts.reshape(rows * HEADS8, width)
        triple = r.frozen_triple
        query_grad = gather_heads(nn(mixed.astype(BF16), triple[:, width : 2 * width]))
        key_grad = jnp.sum((tall_q * self_grad).reshape(rows, HEADS8, width), axis=1)
        value_grad = jnp.sum((tall_low * self_prob).reshape(rows, HEADS8, width), axis=1)
        packed_grad = jnp.concatenate(
            [
                query_grad * HD ** (-0.5),
                r.class_grads[:, 0:width] + key_grad * HD ** (-0.5),
                r.class_grads[:, width:] + value_grad,
            ],
            axis=1,
        ).astype(BF16)
        first_grad = nt(packed_grad, triple[...])
        back = norm_back(first_grad * gain_row, unit, inverse, 1)
        r.class_gradient[...] = (r.middle_grad[...] + back).astype(BF16)
        if dims.inside:
            wide = width * 4 + dims.hidden
            r.region_output[...] = r.region_out[...]
            r.triple_gradient[...] = r.grads_out[:, 0 : 3 * width]
            r.merge_gradient[...] = r.grads_out[:, 3 * width : 4 * width]
            r.expand_gradient[...] = r.grads_out[:, 4 * width : wide]
            r.shrink_gradient[...] = r.shrink_out[...]
            shard = r.grads_out.shape[0]
            blank = jnp.zeros((128 - shard, 128), F32)
            for k, target in enumerate((r.first_gradient, r.second_gradient)):
                columns = r.grads_out[:, wide + 128 * k : wide + 128 * (k + 1)]
                columns = jnp.concatenate([columns, blank], axis=0).T
                target[...] = columns[0:1, 0:shard]


def normalize(values, scaling):
    centred = values - jnp.mean(values, axis=-1, keepdims=True)
    inverse = lax.rsqrt(jnp.mean(centred * centred, axis=-1, keepdims=True) + EPSILON)
    standard = centred * inverse
    return (standard * scaling, standard, inverse)


def normalize_back(upstream, standard, inverse, scaling):
    scaled = upstream * scaling
    centred = scaled - jnp.mean(scaled, axis=-1, keepdims=True)
    centred = centred - standard * jnp.mean(scaled * standard, axis=-1, keepdims=True)
    gain_grad = jnp.sum((upstream * standard).reshape(-1, upstream.shape[-1]), axis=0)
    return (centred * inverse, gain_grad)


def gelu_slope(hidden):
    return (
        0.5 * (1.0 + lax.erf(hidden * 0.7071067811865476))
        + hidden * jnp.exp(-0.5 * hidden * hidden) * 0.3989422804014327
    )


def forward_product(operand, weight):
    return lax.dot_general(
        operand, weight, (((operand.ndim - 1,), (0,)), ((), ())), preferred_element_type=F32
    )


def backward_product(upstream, weight):
    return lax.dot_general(
        upstream,
        weight,
        (((upstream.ndim - 1,), (1,)), ((), ())),
        preferred_element_type=F32,
    )


def row_product(operand, cotangent):
    left_rows = operand.reshape(-1, operand.shape[-1])
    right_rows = cotangent.reshape(-1, cotangent.shape[-1])
    return lax.dot_general(
        left_rows, right_rows, (((0,), (0,)), ((), ())), preferred_element_type=F32
    )


def heads_of(packed, portion):
    section_width = packed.shape[-1] // 3
    section = packed[..., portion * section_width : (portion + 1) * section_width]
    return section.reshape(packed.shape[:-1] + (section_width // HD, HD))


def raw_scores(queries, keyset, allowed):
    scores = jnp.einsum(
        "bqhd,bkhd->bhqk", queries, keyset, preferred_element_type=F32
    ) * HD ** (-0.5)
    if allowed is None:
        return scores
    return jnp.where(allowed[:, None], scores, -1e30)


def attend(queries, keyset, valueset, allowed):
    scores = raw_scores(queries, keyset, allowed)
    highest = jnp.max(scores, axis=-1, keepdims=True)
    logsum = highest + jnp.log(jnp.sum(jnp.exp(scores - highest), axis=-1, keepdims=True))
    weighting = jnp.exp(scores - logsum).astype(BF16)
    context = jnp.einsum("bhqk,bkhd->bqhd", weighting, valueset, preferred_element_type=F32)
    return (context.astype(BF16), logsum)


def score_terms(queries, keyset, valueset, allowed, logsum, context_grad):
    scores = raw_scores(queries, keyset, allowed)
    weighting = jnp.exp(scores - logsum)
    weight_grad = jnp.einsum(
        "bqhd,bkhd->bhqk", context_grad, valueset, preferred_element_type=F32
    )
    row_total = jnp.sum(weighting * weight_grad, axis=-1, keepdims=True)
    score_grad = (weighting * (weight_grad - row_total)).astype(BF16)
    return (weighting, score_grad, row_total)


def attend_back(queries, keyset, valueset, allowed, logsum, context_grad):
    weighting, score_grad, row_total = score_terms(
        queries, keyset, valueset, allowed, logsum, context_grad
    )
    value_grad = jnp.einsum(
        "bhqk,bqhd->bkhd",
        weighting.astype(BF16),
        context_grad,
        preferred_element_type=F32,
    )
    query_grad = jnp.einsum(
        "bhqk,bkhd->bqhd", score_grad, keyset, preferred_element_type=F32
    ) * HD ** (-0.5)
    key_grad = jnp.einsum(
        "bhqk,bqhd->bkhd", score_grad, queries, preferred_element_type=F32
    ) * HD ** (-0.5)
    return (query_grad, key_grad, value_grad)


def block_head(inputs, scaling, triple):
    normed, standard, inverse = normalize(inputs, scaling)
    first_low = normed.astype(BF16)
    packed = forward_product(first_low, triple).astype(BF16)
    return (first_low, standard, inverse, packed)


def block_tail(inputs, context, regain, merger, expand, shrink):
    middle = inputs + forward_product(context, merger)
    normed, standard, inverse = normalize(middle, regain)
    second = normed.astype(BF16)
    hidden = forward_product(second, expand)
    active = jax.nn.gelu(hidden, approximate=False).astype(BF16)
    result = middle + forward_product(active, shrink)
    return (result, (standard, inverse, second, hidden, active))


def tail_back(upstream, kept_tail, regain, merger, expand, shrink):
    standard, inverse, second, hidden, active = kept_tail
    out_low = upstream.astype(BF16)
    active_grad = backward_product(out_low, shrink)
    hidden_low = (active_grad * gelu_slope(hidden)).astype(BF16)
    second_grad = backward_product(hidden_low, expand)
    norm_grad, regain_grad = normalize_back(second_grad, standard, inverse, regain)
    middle_grad = upstream + norm_grad
    middle_low = middle_grad.astype(BF16)
    context_low = backward_product(middle_low, merger).astype(BF16)
    return (middle_grad, context_low, regain_grad, (middle_low, hidden_low, out_low))


def region_outside(crossed, region_number, region_cotangent, shards_in):
    crossed = lax.ppermute(crossed, SEG, [(0, 1), (1, 0)])
    images = crossed.shape[1]
    model_width = crossed.shape[2]
    gathered = [lax.all_gather(shard, IMG, axis=0, tiled=True) for shard in shards_in]
    full_gain, triple, merger, full_regain, expand, shrink = gathered
    scaling = full_gain.astype(F32)
    regain = full_regain.astype(F32)
    region_in = crossed.astype(F32)
    first_low, standard, inverse, packed = block_head(region_in, scaling, triple)
    local_keys = packed[..., model_width : 2 * model_width]
    local_values = packed[..., 2 * model_width :]
    all_keys, all_values = (
        lax.all_gather(local_keys, IMG, axis=1, tiled=True),
        lax.all_gather(local_values, IMG, axis=1, tiled=True),
    )
    head_shape = all_keys.shape[:-1] + (model_width // HD, HD)
    keyset = all_keys.reshape(head_shape)
    valueset = all_values.reshape(head_shape)
    queries = heads_of(packed, 0)
    first_slot = lax.axis_index(IMG) * images
    own_number = lax.dynamic_slice_in_dim(region_number, first_slot, images, 1)
    allowed = own_number[:, :, None] == region_number[:, None, :]
    context, logsum = attend(queries, keyset, valueset, allowed)
    context = context.reshape(region_in.shape)
    region_result, kept_tail = block_tail(region_in, context, regain, merger, expand, shrink)
    region_output = region_result.astype(BF16)
    upstream = region_cotangent.astype(F32)
    middle_grad, context_low, second_gain_grad, low_rows = tail_back(
        upstream, kept_tail, regain, merger, expand, shrink
    )
    middle_low, hidden_low, out_low = low_rows
    context_heads = context_low.reshape(queries.shape)
    query_grad, key_grad, value_grad = attend_back(
        queries, keyset, valueset, allowed, logsum, context_heads
    )
    key_sum, value_sum = (
        lax.psum_scatter(key_grad.reshape(all_keys.shape), IMG, scatter_dimension=1, tiled=True),
        lax.psum_scatter(
            value_grad.reshape(all_values.shape), IMG, scatter_dimension=1, tiled=True
        ),
    )
    packed_grad = jnp.concatenate(
        [query_grad.reshape(region_in.shape), key_sum, value_sum], axis=-1
    ).astype(BF16)
    norm_grad, first_gain_grad = normalize_back(
        backward_product(packed_grad, triple), standard, inverse, scaling
    )
    input_grad = (middle_grad + norm_grad).astype(BF16)
    second_low = kept_tail[2]
    active_low = kept_tail[4]
    shards = (
        lax.psum_scatter(first_gain_grad, IMG, scatter_dimension=0, tiled=True),
        lax.psum_scatter(
            row_product(first_low, packed_grad), IMG, scatter_dimension=0, tiled=True
        ),
        lax.psum_scatter(row_product(context, middle_low), IMG, scatter_dimension=0, tiled=True),
        lax.psum_scatter(second_gain_grad, IMG, scatter_dimension=0, tiled=True),
        lax.psum_scatter(
            row_product(second_low, hidden_low), IMG, scatter_dimension=0, tiled=True
        ),
        lax.psum_scatter(row_product(active_low, out_low), IMG, scatter_dimension=0, tiled=True),
    )
    totals = tuple(lax.psum(shard.astype(BF16), SEG).astype(F32) for shard in shards)
    return region_output, lax.ppermute(input_grad, SEG, [(0, 1), (1, 0)]), totals


def local(
    n_img,
    patch_tokens,
    class_tokens,
    region_number,
    frozen_gain,
    frozen_triple,
    frozen_merge,
    frozen_regain,
    frozen_expand,
    frozen_shrink,
    gain_first,
    weight_triple,
    weight_merge,
    gain_second,
    weight_expand,
    weight_shrink,
    patch_cotangent,
    region_cotangent,
):
    micros, per, patches, width = patch_tokens.shape
    hidden = frozen_expand.shape[1]
    images = micros * per
    shard, shard_ff = width // n_img, hidden // n_img
    lanes, pairs, keys, heads = 2 * patches, images // 2, n_img * images, width // HD
    inside = keys == patches and shard % 8 == 0 and shard <= PAD

    vectors = [frozen_gain, frozen_regain]
    if inside:
        vectors += [jnp.pad(g, (0, 128 - shard)) for g in (gain_first, gain_second)]
    vectors = jnp.concatenate(vectors)
    vectors = jnp.pad(vectors, (0, 1024 - vectors.shape[0])).astype(F32).reshape(8, 128)
    class_rows = class_tokens.reshape(images, width)
    inputs = dict(
        tokens=patch_tokens.reshape(images, patches, width),
        cotangent=patch_cotangent.reshape(images, patches, width),
        class_tokens=class_rows,
        vectors=vectors,
        frozen_triple=frozen_triple,
        frozen_merge=frozen_merge,
        frozen_expand=frozen_expand,
        frozen_shrink=frozen_shrink,
    )
    if inside:
        inputs |= dict(
            region_cotangent=region_cotangent.reshape(images, width),
            region_number=region_number,
            weight_triple=weight_triple,
            weight_merge=weight_merge,
            weight_expand=weight_expand,
            weight_shrink=weight_shrink,
        )
    vmem = pl.BlockSpec(memory_space=pltpu.VMEM)
    hbm = pl.BlockSpec(memory_space=pl.ANY)
    streams = 2
    in_specs = [hbm] * streams + [vmem] * (len(inputs) - streams)

    shape = jax.ShapeDtypeStruct
    columns = 4 * width + hidden + 256
    large = dict(
        patch_rows=shape((images, patches, width), BF16),
        first_rows=shape((pairs, width, lanes), BF16),
        grad_rows=shape((pairs, width, lanes), BF16),
    )
    small = dict(
        stat=shape((pairs, 8, lanes), F32),
        class_packed=shape((images, 3 * width), F32),
        class_context=shape((images, width), F32),
        class_middle=shape((images, width), F32),
        class_slope=shape((images, hidden), F32),
        query_map=shape((images, HEADS8, width), F32),
        class_probs=shape((images, HEADS8, patches), F32),
        self_prob=shape((images, HEADS8, 128), F32),
        class_grads=shape((images, 2 * width), F32),
    )
    if inside:
        small |= dict(
            class_up=shape((images, width), BF16),
            region_out=shape((images, width), BF16),
            grads_out=shape((shard, columns), F32),
            shrink_out=shape((shard_ff, width), F32),
        )
    else:
        small |= dict(class_out=shape((images, width), BF16))
    outputs = large | small
    out_specs = [hbm] * len(large) + [vmem] * len(small)

    v = pltpu.VMEM
    dma = pltpu.SemaphoreType.DMA
    scratch = dict(
        tok=v((images, patches, width), BF16),
        cot=v((images, patches, width), BF16),
        firstT=v((pairs, width, lanes), BF16),
        input_grad=v((pairs, width, lanes), BF16),
        tripleT=v((3 * width, width), BF16),
        mergeT=v((width, width), BF16),
        expandT=v((hidden, width), BF16),
        shrinkT=v((width, hidden), BF16),
        gainT=v((width, lanes), F32),
        regainT=v((width, lanes), F32),
        qkv=v((3 * width, lanes), BF16),
        ctx=v((width, lanes), BF16),
        probs=v((2 * heads, patches, patches), BF16),
        shares=v((2, HEADS8, patches), F32),
        class_weights=v((2, HEADS8, patches), F32),
        active=v((hidden, lanes), BF16),
        slope=v((hidden, lanes), BF16),
        packed_grad=v((3 * width, lanes), BF16),
        low_grad=v((width, lanes), BF16),
        class_k=v((images, HEADS8, width), F32),
        class_v=v((images, HEADS8, width), F32),
        class_dk=v((images, HEADS8, width), F32),
        class_dv=v((images, HEADS8, width), F32),
        class_first=v((images, HEADS8, width), F32),
        mixed=v((images, HEADS8, width), F32),
        self_score=v((images, HEADS8, 128), F32),
        tok_sem=dma((pairs,)),
        cot_sem=dma((pairs,)),
        out_sem=dma((pairs,)),
        first_sem=dma((pairs,)),
        grad_sem=dma((pairs,)),
    )
    if inside:
        deep = PAD * n_img
        scratch |= dict(
            class_out=v((images, width), BF16),
            crossed=v((n_img, images, width), BF16),
            crossed_grad=v((images, width), BF16),
            returned=v((images, width), BF16),
            region_up=v((n_img, images, width), BF16),
            gain_own=v((2 * shard, 128), F32),
            gains=v((n_img, 2 * shard, 128), F32),
            w_own=v((2, PAD, 4 * width), BF16),
            w_all=v((2, n_img, PAD, 4 * width), BF16),
            s_own=v((2, shard_ff // 2, width), BF16),
            s_all=v((2, n_img, shard_ff // 2, width), BF16),
            region_shrink=v((hidden, width), BF16),
            region_first=v((deep, keys), BF16),
            region_context=v((deep, keys), BF16),
            region_second=v((deep, keys), BF16),
            region_active=v((hidden, keys), BF16),
            region_rows=v((keys, width), F32),
            gain_columns=v((width, 128), F32),
            grads=v((shard, columns), F32),
            grads_in=v((shard, columns), F32),
            grads_shrink=v((shard_ff, width), F32),
            grads_shrink_in=v((shard_ff, width), F32),
            l_gain=dma((2,)),
            l_up=dma((2,)),
            l_weights=dma((2,)),
            l_shrink=dma((2,)),
            l_forward=dma((2,)),
            l_forward_shrink=dma((2,)),
            l_crossed=dma((2,)),
            l_returned=dma((2,)),
            l_grads=dma((2,)),
            l_grads_shrink=dma((2,)),
        )
    sizes = dict(
        n_img=n_img, width=width, hidden=hidden, images=images, patches=patches, inside=inside
    )
    limit = dict(vmem_limit_bytes=60 * 1024 * 1024)
    remote = dict(collective_id=0, has_side_effects=True) if inside else {}
    names = list(inputs) + list(outputs) + list(scratch)
    results = pl.pallas_call(
        functools.partial(patch_kernel, SimpleNamespace(names=names, **sizes)),
        out_shape=list(outputs.values()),
        in_specs=in_specs,
        out_specs=out_specs,
        scratch_shapes=list(scratch.values()),
        compiler_params=pltpu.CompilerParams(**limit, **remote),
    )(*inputs.values())
    done = dict(zip(outputs, results, strict=True))

    if not inside:
        class_out = done.pop(list(small)[-1])
        region_output, class_up, grads = region_outside(
            class_out.reshape(class_tokens.shape),
            region_number,
            region_cotangent,
            (gain_first, weight_triple, weight_merge, gain_second, weight_expand, weight_shrink),
        )
        done |= dict(class_up=class_up.reshape(images, width))

    def step(*block):
        return pl.BlockSpec(block, lambda it: (it,) + (0,) * (len(block) - 1))

    specs = dict(
        patch_rows=step(2, patches, width),
        first_rows=step(1, width, lanes),
        grad_rows=step(1, width, lanes),
        stat=step(1, 8, lanes),
        query_map=step(2, HEADS8, width),
        class_probs=step(2, HEADS8, patches),
    )
    inputs = done | dict(
        class_tokens=class_rows,
        vectors=vectors,
        frozen_triple=frozen_triple,
        frozen_merge=frozen_merge,
        frozen_expand=frozen_expand,
        frozen_shrink=frozen_shrink,
    )
    outputs = dict(
        patch_output=shape((images, patches, width), BF16),
        patch_gradient=shape((images, patches, width), BF16),
        class_gradient=shape((images, width), BF16),
    )
    out_specs = [step(2, patches, width)] * 2 + [vmem]
    if inside:
        ready = dict(
            region_output=shape((images, width), BF16),
            first_gradient=shape((1, shard), F32),
            triple_gradient=shape((shard, 3 * width), F32),
            merge_gradient=shape((shard, width), F32),
            second_gradient=shape((1, shard), F32),
            expand_gradient=shape((shard, hidden), F32),
            shrink_gradient=shape((shard_ff, width), F32),
        )
        outputs |= ready
        out_specs += [vmem] * len(ready)
    scratch = dict(
        gainT=v((width, lanes), F32),
        ungainT=v((width, lanes), F32),
        middle_grad=v((images, width), F32),
        class_low=v((images, width), F32),
        low_map=v((images, HEADS8, width), F32),
        class_total=v((images, HEADS8, 128), F32),
        mixed=v((images, HEADS8, width), F32),
    )
    names = list(inputs) + list(outputs) + list(scratch)
    results = pl.pallas_call(
        functools.partial(class_kernel, SimpleNamespace(names=names, **sizes)),
        grid=(pairs,),
        out_shape=list(outputs.values()),
        in_specs=[specs.get(name, vmem) for name in inputs],
        out_specs=out_specs,
        scratch_shapes=list(scratch.values()),
        compiler_params=pltpu.CompilerParams(**limit),
    )(*inputs.values())
    done = SimpleNamespace(**dict(zip(outputs, results, strict=True)))
    if inside:
        region_output = done.region_output.reshape(class_tokens.shape)
        grads = (
            done.first_gradient.reshape(shard),
            done.triple_gradient,
            done.merge_gradient,
            done.second_gradient.reshape(shard),
            done.expand_gradient,
            done.shrink_gradient,
        )
    return (
        done.patch_output.reshape(patch_tokens.shape),
        region_output,
        done.patch_gradient.reshape(patch_tokens.shape),
        done.class_gradient.reshape(class_tokens.shape),
        *grads,
    )


def solution(mesh):
    patch, row = P(SEG, IMG, None, None), P(SEG, IMG, None)
    gain, weight, whole = P(IMG), P(IMG, None), P()
    block = (gain, weight, weight, gain, weight, weight)
    placed = (patch, row, P(SEG, None)) + (whole,) * 6 + block + (patch, row)
    return jax.shard_map(
        functools.partial(local, mesh.shape[IMG]),
        mesh=mesh,
        in_specs=placed,
        out_specs=(patch, row, patch, row) + block,
        check_vma=False,
    )
```

time: 1230 us -> 128 us (0.10)
  waiting for transfers between devices: 539 us -> 0 us
  matrix products: 275 us -> 0 us
  blocking collectives: 239 us -> 0 us
  Pallas kernels: 0 us -> 126 us
  other arithmetic: 85.8 us -> 1.33 us
  local copies, waits for them, and re-layouts: 66.9 us -> 0 us
  between operations: 16.7 us -> 0.81 us
    reduce_scatter x4 -> x0, waiting for transfers between devices: 502 us -> none  [the longest x1 131 us: local(): lax.psum_scatter(row_product(second_low, hidden_low), 'img', scatter_dime...]
    dot_general x32 -> x0, matrix products: 275 us -> none  [the longest x8 100 us: forward_product(): lax.dot_general(operand, weight, (((operand.ndim - 1,), (0,)), ((), ())),...]
    all_gather x4 -> x0, blocking collectives: 161 us -> none  [the longest x1 48.2 us: local(): lax.all_gather(weight_triple, 'img', axis=0, tiled=True)]
    pallas_call x0 -> x2, Pallas kernels: none -> 126 us  [the longest x1 111 us: local(): pl.pallas_call(functools.partial(patch_kernel, SimpleNamespace(names=name...]
    unnamed x2 -> x0, blocking collectives: 78.6 us -> none
    convert_element_type x17 -> x1, other arithmetic: 48.2 us -> 1.33 us  [local(): jnp.pad(vectors, (0, 1024 - vectors.shape[0])).astype(F32).reshape(8, 128)]
    slice x9 -> x0, local copies, waits for them, and re-layouts: 30.4 us -> none  [the longest x5 22.5 us: heads_of(): section = packed[..., portion * section_width:(portion + 1) * section_width]]
    reduce_sum x8 -> x0, other arithmetic: 25.4 us -> none  [the longest x2 16.9 us: attend(): jnp.sum(jnp.exp(scores - highest), axis=-1, keepdims=True)]
  transfers between devices with their start and end apart: 12 -> 0, of which waited for: 7 -> 0; matrix products, arithmetic and copies ran while one was open for 34% -> 0% of each run, Pallas kernels for 0% -> 0%
where the time goes in v1:
time: 128 us
  Pallas kernels  126 us (98%)
  other arithmetic  1.33 us (1%)
    pallas_call x1, Pallas kernels, local(): pl.pallas_call(functools.partial(patch_kernel, SimpleNamespace(names=name...  111 us
    pallas_call x1, Pallas kernels, local(): pl.pallas_call(functools.partial(class_kernel, SimpleNamespace(names=name...  15.4 us

profile of v1, /device:TPU:0, one launch (start us, length us, event | category | flops | bytes accessed | tf_op | source)
XLA Modules:
  0.0 128.1 jit_solution(1069992729270087809)
XLA Ops:
  0.6 1.3 %fusion.6.refs_3_.refs_17_ = f32[8,128]{1,0:T(8,128)} fusion(bf16[24]{0:T(256)(128)(2,1)} %param.29, bf16[24]{0:T(256)(128)(2,1)} %param.26, bf16[384]{0:T(512)(128)(2,1)} %param.23, bf16[384]{0:T(512)(128)(2,1)} %param.20), kind=kLoop, calls=%fused_computation.9 | loop fusion | flops 15360 | bytes 5728 | tf_op jit(solution)/shard_map/convert_element_type | solution.py:866
  2.0 110.5 %shard_map.240 = (bf16[16,256,384]{2,1,0:T(8,128)(2,1)}, bf16[8,384,512]{2,1,0:T(8,128)(2,1)}, bf16[8,384,512]{2,1,0:T(8,128)(2,1)}, f32[8,8,512]{2,1,0:T(8,128)...) custom-call(bf16[16,256,384]{2,1,0:T(8,128)(2,1)} %bitcast.15, ...), custom_call_target="tpu_custom_call" | custom-call | tf_op jit(solution)/shard_map/pallas_call | solution.py:999
  112.5 15.4 %shard_map.241 = (bf16[16,256,384]{2,1,0:T(8,128)(2,1)}, bf16[16,256,384]{2,1,0:T(8,128)(2,1)}, bf16[16,384]{1,0:T(8,128)(2,1)}, bf16[16,384]{1,0:T(8,128)(2,1)}...) custom-call(bf16[16,256,384]{2,1,0:T(8,128)(2,1)} %get-tuple-element, ...), custom_call_target="tpu_custom_call" | custom-call | tf_op jit(solution)/shard_map/pallas_call | solution.py:1066

commit v2 on v1

--- a/solution.py
+++ b/solution.py
@@ -22,9 +22,11 @@
 MESH = pl.DeviceIdType.MESH
 NEG = -1e30
 PAD = 32
-
-AT_FORWARD = 6
-AT_REGION = 7
+BESIDE = "_"
+
+AT_FORWARD = 5
+AT_REGION = 6
+LATE = 1
 
 
 def nn(a, b):
@@ -92,6 +94,10 @@
 def pair_copy(source, target, sems, it):
     part = pl.ds(2 * it, 2)
     return pltpu.make_async_copy(source.at[part], target.at[part], sems.at[it])
+
+
+def one_copy(source, target, sems, it):
+    return pltpu.make_async_copy(source.at[it], target.at[it], sems.at[it])
 
 
 def padded(values, shard, n):
@@ -104,6 +110,130 @@
 
 def trimmed(values, shard, n):
     return jnp.concatenate([values[PAD * j : PAD * j + shard] for j in range(n)], axis=0)
+
+
+def patch_pair(r, dims, it, slot, ready=lambda stage: None):
+    width, hidden, patches = dims.width, dims.hidden, dims.patches
+    heads = width // HD
+    block_head = own_heads(1, width)
+    span = [slice(b * patches, (b + 1) * patches) for b in range(2)]
+    qkv, ctx, probs = r.qkv, r.ctx, r.probs
+    values = jnp.concatenate([r.tok[2 * slot + b].T for b in range(2)], axis=1).astype(F32)
+    ready(0)
+    first = r.firstT[it]
+    queries = nn(r.tripleT[0:width, :], first) * (LOG2E * HD ** (-0.5))
+    qkv[0:width, :] = queries.astype(BF16)
+    qkv[width:, :] = nn(r.tripleT[width:, :], first).astype(BF16)
+    order = [(b, h) for h in range(heads) for b in range(2)]
+    key_rows = [r.class_k[2 * it + b].astype(BF16) for b in range(2)]
+    value_rows = [r.class_v[2 * it + b].astype(BF16) for b in range(2)]
+    class_scores = [nn(key_rows[b], qkv[0:width, span[b]]) for b in range(2)]
+
+    def part(which, turn):
+        b, h = order[turn]
+        return qkv[which * width + HD * h : which * width + HD * (h + 1), span[b]]
+
+    scores, mixes, class_weights, shares = {0: tn(part(1, 0), part(0, 0))}, [], [], []
+    for turn, (b, h) in enumerate(order):
+        if turn + 1 < len(order):
+            scores[turn + 1] = tn(part(1, turn + 1), part(0, turn + 1))
+        class_score = class_scores[b][h : h + 1, :]
+        top = jnp.maximum(jnp.max(scores[turn], axis=0, keepdims=True), class_score)
+        weights = jnp.exp2(scores.pop(turn) - top)
+        class_weight = jnp.exp2(class_score - top)
+        shares.append(1.0 / (jnp.sum(weights, axis=0, keepdims=True) + class_weight))
+        class_weights.append(class_weight)
+        probs[b * heads + h] = weights.astype(BF16)
+        if turn:
+            last = order[turn - 1]
+            mixes.append(nn(part(2, turn - 1), probs[last[0] * heads + last[1]]))
+    mixes.append(nn(part(2, len(order) - 1), probs[2 * heads - 1]))
+    blank = [jnp.zeros((HEADS8 - heads, patches), F32)]
+    for b in range(2):
+        weights = jnp.concatenate(class_weights[b::2] + blank, axis=0)
+        r.class_weights[b] = weights
+        r.shares[b] = jnp.concatenate(shares[b::2] + blank, axis=0)
+        from_class = tn(value_rows[b], weights.astype(BF16))
+        for h in range(heads):
+            at = slice(HD * h, HD * (h + 1))
+            mix = mixes[2 * h + b] + from_class[at]
+            ctx[at, span[b]] = (mix * shares[2 * h + b]).astype(BF16)
+    ready(1)
+    middle = values + nn(r.mergeT[...], ctx[...])
+    unit_b, _, inverse_b = standardize(middle, 0)
+    second = (unit_b * r.regainT[...]).astype(BF16)
+    chunk = width
+    for c in range(0, hidden, chunk):
+        at = slice(c, c + chunk)
+        active, slope = gelu_pair(nn(r.expandT[at, :], second))
+        r.active[at, :] = active.astype(BF16)
+        r.slope[at, :] = slope.astype(BF16)
+    result = middle + nn(r.shrinkT[...], r.active[...])
+    for b in range(2):
+        r.tok[2 * slot + b] = result[:, span[b]].astype(BF16).T
+    ready(2)
+    upstream = jnp.concatenate([r.cot[2 * slot + b].T for b in range(2)], axis=1)
+    for c in range(0, hidden, chunk):
+        at = slice(c, c + chunk)
+        active_grad = nn(r.frozen_shrink[at, :], upstream)
+        r.active[at, :] = active_grad.astype(BF16) * r.slope[at, :]
+    second_grad = nn(r.frozen_expand[...], r.active[...])
+    middle_grad = upstream.astype(F32) + norm_back(
+        second_grad * r.regainT[...], unit_b, inverse_b, 0
+    )
+    context_grad = nn(r.frozen_merge[...], middle_grad.astype(BF16))
+    low_grad, packed_grad = r.low_grad, r.packed_grad
+    totals, from_class = [[], []], []
+    for b in range(2):
+        for h in range(heads):
+            at = slice(HD * h, HD * (h + 1))
+            low = context_grad[at, span[b]] * r.shares[b][h : h + 1, :]
+            totals[b].append(
+                jnp.sum(low * ctx[at, span[b]].astype(F32), axis=0, keepdims=True)
+            )
+            low_grad[at, span[b]] = low.astype(BF16)
+        all_low = low_grad[:, span[b]]
+        weights = r.class_weights[b]
+        class_grad = weights * (
+            nn(value_rows[b], all_low) - jnp.concatenate(totals[b] + blank, axis=0)
+        )
+        class_grad = class_grad.astype(BF16)
+        from_class.append(tn(key_rows[b], class_grad))
+        dk = nt(class_grad, qkv[0:width, span[b]]) * LN2
+        dv = nt(weights.astype(BF16), all_low)
+        r.class_dk[2 * it + b] = jnp.where(block_head, dk, 0.0)
+        r.class_dv[2 * it + b] = jnp.where(block_head, dv, 0.0)
+
+    def low_part(turn):
+        b, h = order[turn]
+        return low_grad[HD * h : HD * (h + 1), span[b]]
+
+    def put(which, turn, grad):
+        b, h = order[turn]
+        rows_at = slice(which * width + HD * h, which * width + HD * (h + 1))
+        packed_grad[rows_at, span[b]] = grad.astype(BF16)
+
+    def key_and_query(turn, score_grad):
+        b, h = order[turn]
+        put(1, turn, nt(part(0, turn), score_grad) * LN2)
+        query_grad = nn(part(1, turn), score_grad) + from_class[b][HD * h : HD * (h + 1)]
+        put(0, turn, query_grad * HD ** (-0.5))
+
+    grads, score_grads = {0: tn(part(2, 0), low_part(0))}, {}
+    for turn, (b, h) in enumerate(order):
+        if turn + 1 < len(order):
+            grads[turn + 1] = tn(part(2, turn + 1), low_part(turn + 1))
+        weights = probs[b * heads + h]
+        put(2, turn, nt(low_part(turn), weights))
+        score_grads[turn] = weights * (grads.pop(turn) - totals[b][h]).astype(BF16)
+        if turn:
+            key_and_query(turn - 1, score_grads.pop(turn - 1))
+    key_and_query(len(order) - 1, score_grads.pop(len(order) - 1))
+    first_grad = nn(r.frozen_triple[...], packed_grad[...])
+    centre, inverse = r.stat[it, 0:1, :], r.stat[it, 1:2, :]
+    unit = (values - centre) * inverse
+    back = norm_back(first_grad * r.gainT[...], unit, inverse, 0)
+    r.input_grad[it] = (middle_grad + back).astype(BF16)
 
 
 def patch_kernel(dims, *refs):
@@ -178,38 +308,44 @@
 
     for it in range(pairs):
         pair_copy(r.tokens, r.tok, r.tok_sem, it).start()
-    for it in range(pairs):
+    for it in range(dims.early):
         pair_copy(r.cotangent, r.cot, r.cot_sem, it).start()
 
     vectors = r.vectors[...]
     gain_row = wide_row(vectors, 0, width // 128)
     regain_row = wide_row(vectors, width // 128, width // 128)
+    r.tripleT[...] = r.frozen_triple[...].T
+    r.mergeT[...] = r.frozen_merge[...].T
+    r.expandT[...] = r.frozen_expand[...].T
+    r.shrinkT[...] = r.frozen_shrink[...].T
+    turns = (
+        (r.tripleT, r.triple_turned),
+        (r.mergeT, r.merge_turned),
+        (r.expandT, r.expand_turned),
+        (r.shrinkT, r.shrink_turned),
+    )
+    for k, (turned, target) in enumerate(turns):
+        pltpu.make_async_copy(turned, target, r.turn_sem.at[k]).start()
+    r.gainT[...] = column(gain_row, lanes)
+    r.regainT[...] = column(regain_row, lanes)
+
     if inside:
-        blank = jnp.zeros((PAD - shard, 4 * width), F32)
+        upstream = r.region_cotangent[...].astype(F32)
+        fill = [upstream[8 * k : 8 * k + 8] for k in range(rows // 8)]
+        for k in range(2):
+            row = vectors[2 * width // 128 + k : 2 * width // 128 + k + 1, :]
+            tall = column(row, 128)
+            fill += [tall[at : at + 8] for at in range(0, shard, 8)]
+        fill = jnp.concatenate(fill, axis=1)
         triple = r.weight_triple[...].astype(F32)
         merge = r.weight_merge[...].astype(F32)
         expand = r.weight_expand[...].astype(F32)
         first_half = jnp.concatenate([triple, merge], axis=1)
-        r.w_own[0] = jnp.concatenate([first_half, blank], axis=0).astype(BF16)
-        r.w_own[1] = jnp.concatenate([expand, blank], axis=0).astype(BF16)
+        r.w_own[0] = jnp.concatenate([first_half, fill], axis=0).astype(BF16)
+        r.w_own[1] = jnp.concatenate([expand, fill], axis=0).astype(BF16)
         for k in range(2):
             r.s_own[k] = r.weight_shrink[k * shard_ff // 2 : (k + 1) * shard_ff // 2, :]
-            row = vectors[2 * width // 128 + k : 2 * width // 128 + k + 1, :]
-            r.gain_own[k * shard : (k + 1) * shard, :] = column(row, 128)[0:shard]
-        pl.semaphore_wait(barrier, 2 * n_img - 1)
-        to_peers(r.gain_own, r.gains.at[me], r.l_gain)
-        to_peers(r.region_cotangent, r.region_up.at[me], r.l_up)
-        to_peers(r.w_own.at[seg], r.w_all.at[seg, me], r.l_weights)
-        to_peers(r.s_own.at[seg], r.s_all.at[seg, me], r.l_shrink)
-
-    r.tripleT[...] = r.frozen_triple[...].T
-    r.mergeT[...] = r.frozen_merge[...].T
-    r.expandT[...] = r.frozen_expand[...].T
-    r.shrinkT[...] = r.frozen_shrink[...].T
-    r.gainT[...] = column(gain_row, lanes)
-    r.regainT[...] = column(regain_row, lanes)
-
-    block_head = own_heads(1, width)
+
     class_in = r.class_tokens[...].astype(F32)
     class_unit, _, _ = standardize(class_in, 1)
     class_first = (class_unit * gain_row).astype(BF16)
@@ -243,6 +379,7 @@
         scores = nn(maps.astype(BF16), first)
         for b in range(2):
             part = scores[b * HEADS8 : (b + 1) * HEADS8, b * patches : (b + 1) * patches]
+            r.class_scores[2 * it + b] = part
             alone = r.self_score[2 * it + b][:, 0:1]
             top = jnp.maximum(jnp.max(part, axis=1, keepdims=True), alone)
             weights = jnp.exp2(part - top)
@@ -256,7 +393,12 @@
             r.mixed[2 * it + b] = mixed + weight_alone * r.class_first[2 * it + b]
         return carry
 
-    lax.fori_loop(0, pairs, class_forward, 0)
+    lax.fori_loop(0, pairs // 2, class_forward, 0, unroll=2)
+    if inside:
+        pl.semaphore_wait(barrier, 2 * n_img - 1)
+        to_peers(r.w_own.at[seg], r.w_all.at[seg, me], r.l_weights)
+        to_peers(r.s_own.at[seg], r.s_all.at[seg, me], r.l_shrink)
+    lax.fori_loop(pairs // 2, pairs, class_forward, 0, unroll=2)
 
     mixed = r.mixed[...].reshape(rows * HEADS8, width).astype(BF16)
     class_context = gather_heads(nn(mixed, r.frozen_triple[:, 2 * width :])).astype(BF16)
@@ -274,8 +416,6 @@
 
     def region():
         keys = n_img * rows
-        wait_all(r.gains, r.l_gain.at[1])
-        wait_all(r.region_up, r.l_up.at[1])
         wait_all(r.crossed, r.l_crossed.at[1])
         sibling(r.w_all.at[seg], r.w_all.at[seg], r.l_forward).wait()
         sibling(r.s_all.at[seg], r.s_all.at[seg], r.l_forward_shrink).wait()
@@ -288,8 +428,17 @@
         w_triple = r.w_all[0, :, :, 0 : 3 * width].reshape(deep, 3 * width)
         w_merge = r.w_all[0, :, :, 3 * width :].reshape(deep, width)
         w_expand = r.w_all[1].reshape(deep, hidden)
-        wide = [r.gains[:, k * shard : (k + 1) * shard, :].reshape(width, 128) for k in range(2)]
+        ups, wide = [], [[], []]
+        for j in range(n_img):
+            fill = r.w_all[seg, j].astype(F32)[shard:PAD]
+            ups += [fill[:, width * k : width * (k + 1)] for k in range(rows // 8)]
+            for k in range(2):
+                first_at = width * (rows // 8) + 128 * (shard // 8) * k
+                for at in range(first_at, first_at + 128 * (shard // 8), 128):
+                    wide[k].append(fill[:, at : at + 128])
+        wide = [jnp.concatenate(w, axis=0) for w in wide]
         gain, regain = (jnp.concatenate([g] * (keys // 128), axis=1) for g in wide)
+        upstream = jnp.concatenate(ups, axis=0).T.astype(BF16)
 
         slots = r.region_number.shape[1]
         per = slots // n_img
@@ -342,7 +491,6 @@
         r.region_rows[...] = result.T
         r.region_out[...] = r.region_rows[mine, :].astype(BF16)
 
-        upstream = r.region_up[...].reshape(keys, width).T
         for c in range(0, hidden, width):
             at = slice(c, c + width)
             active_grad = nn(r.region_shrink[at, :], upstream)
@@ -392,113 +540,11 @@
         sibling(grads, r.grads_in, r.l_grads).start()
         sibling(r.grads_shrink, r.grads_shrink_in, r.l_grads_shrink).start()
 
-    def patch_pair(it, carry):
-        span = [slice(b * patches, (b + 1) * patches) for b in range(2)]
-        qkv, ctx, probs = r.qkv, r.ctx, r.probs
-        values = jnp.concatenate([r.tok[2 * it + b].T for b in range(2)], axis=1).astype(F32)
-        first = r.firstT[it]
-        queries = nn(r.tripleT[0:width, :], first) * (LOG2E * HD ** (-0.5))
-        qkv[0:width, :] = queries.astype(BF16)
-        qkv[width:, :] = nn(r.tripleT[width:, :], first).astype(BF16)
-        for b in range(2):
-            key_row = r.class_k[2 * it + b].astype(BF16)
-            value_row = r.class_v[2 * it + b].astype(BF16)
-            class_scores = nn(key_row, qkv[0:width, span[b]])
-            mixes, class_weights, shares = [], [], []
-            for h in range(heads):
-                q = qkv[HD * h : HD * (h + 1), span[b]]
-                k = qkv[width + HD * h : width + HD * (h + 1), span[b]]
-                v = qkv[2 * width + HD * h : 2 * width + HD * (h + 1), span[b]]
-                scores = tn(k, q)
-                class_score = class_scores[h : h + 1, :]
-                top = jnp.maximum(jnp.max(scores, axis=0, keepdims=True), class_score)
-                weights = jnp.exp2(scores - top)
-                class_weight = jnp.exp2(class_score - top)
-                share = 1.0 / (jnp.sum(weights, axis=0, keepdims=True) + class_weight)
-                low = weights.astype(BF16)
-                probs[b * heads + h] = low
-                mixes.append(nn(v, low))
-                class_weights.append(class_weight)
-                shares.append(share)
-            blank = [jnp.zeros((HEADS8 - heads, patches), F32)]
-            class_weights = jnp.concatenate(class_weights + blank, axis=0)
-            r.class_weights[b] = class_weights
-            r.shares[b] = jnp.concatenate(shares + blank, axis=0)
-            from_class = tn(value_row, class_weights.astype(BF16))
-            for h in range(heads):
-                at = slice(HD * h, HD * (h + 1))
-                ctx[at, span[b]] = ((mixes[h] + from_class[at]) * shares[h]).astype(BF16)
-        middle = values + nn(r.mergeT[...], ctx[...])
-        unit_b, _, inverse_b = standardize(middle, 0)
-        second = (unit_b * r.regainT[...]).astype(BF16)
-        chunk = width
-        for c in range(0, hidden, chunk):
-            at = slice(c, c + chunk)
-            active, slope = gelu_pair(nn(r.expandT[at, :], second))
-            r.active[at, :] = active.astype(BF16)
-            r.slope[at, :] = slope.astype(BF16)
-        result = middle + nn(r.shrinkT[...], r.active[...])
-        for b in range(2):
-            r.tok[2 * it + b] = result[:, span[b]].astype(BF16).T
+    def one_pair(it, carry):
+        pair_copy(r.cotangent, r.cot, r.cot_sem, it).wait()
+        patch_pair(r, dims, it, it)
         pair_copy(r.tok, r.patch_rows, r.out_sem, it).start()
-        pair_copy(r.cotangent, r.cot, r.cot_sem, it).wait()
-        upstream = jnp.concatenate([r.cot[2 * it + b].T for b in range(2)], axis=1)
-        for c in range(0, hidden, chunk):
-            at = slice(c, c + chunk)
-            active_grad = nn(r.frozen_shrink[at, :], upstream)
-            r.active[at, :] = active_grad.astype(BF16) * r.slope[at, :]
-        second_grad = nn(r.frozen_expand[...], r.active[...])
-        middle_grad = upstream.astype(F32) + norm_back(
-            second_grad * r.regainT[...], unit_b, inverse_b, 0
-        )
-        context_grad = nn(r.frozen_merge[...], middle_grad.astype(BF16))
-        low_grad, packed_grad = r.low_grad, r.packed_grad
-        for b in range(2):
-            key_row = r.class_k[2 * it + b].astype(BF16)
-            value_row = r.class_v[2 * it + b].astype(BF16)
-            totals = []
-            for h in range(heads):
-                at = slice(HD * h, HD * (h + 1))
-                part = context_grad[at, span[b]] * r.shares[b][h : h + 1, :]
-                totals.append(
-                    jnp.sum(part * ctx[at, span[b]].astype(F32), axis=0, keepdims=True)
-                )
-                low_grad[at, span[b]] = part.astype(BF16)
-            blank = [jnp.zeros((HEADS8 - heads, patches), F32)]
-            all_low = low_grad[:, span[b]]
-            class_weights = r.class_weights[b]
-            class_grad = class_weights * (
-                nn(value_row, all_low) - jnp.concatenate(totals + blank, axis=0)
-            )
-            class_grad = class_grad.astype(BF16)
-            from_class = tn(key_row, class_grad)
-            dk = nt(class_grad, qkv[0:width, span[b]]) * LN2
-            dv = nt(class_weights.astype(BF16), all_low)
-            r.class_dk[2 * it + b] = jnp.where(block_head, dk, 0.0)
-            r.class_dv[2 * it + b] = jnp.where(block_head, dv, 0.0)
-            for h in range(heads):
-                at = slice(HD * h, HD * (h + 1))
-                q = qkv[at, span[b]]
-                k = qkv[width + HD * h : width + HD * (h + 1), span[b]]
-                v = qkv[2 * width + HD * h : 2 * width + HD * (h + 1), span[b]]
-                low = low_grad[at, span[b]]
-                weights = probs[b * heads + h]
-                score_grad = weights * (tn(v, low) - totals[h]).astype(BF16)
-                value_grad = nt(low, weights)
-                key_grad = nt(q, score_grad) * LN2
-                query_grad = (nn(k, score_grad) + from_class[at]) * HD ** (-0.5)
-                packed_grad[at, span[b]] = query_grad.astype(BF16)
-                packed_grad[width + HD * h : width + HD * (h + 1), span[b]] = key_grad.astype(BF16)
-                packed_grad[2 * width + HD * h : 2 * width + HD * (h + 1), span[b]] = (
-                    value_grad.astype(BF16)
-                )
-        first_grad = nn(r.frozen_triple[...], packed_grad[...])
-        centre, inverse = r.stat[it, 0:1, :], r.stat[it, 1:2, :]
-        unit = (values - centre) * inverse
-        back = norm_back(first_grad * r.gainT[...], unit, inverse, 0)
-        r.input_grad[it] = (middle_grad + back).astype(BF16)
-
-        pltpu.make_async_copy(r.input_grad.at[it], r.grad_rows.at[it], r.grad_sem.at[it]).start()
+        one_copy(r.input_grad, r.grad_rows, r.grad_sem, it).start()
 
         if inside:
 
@@ -513,11 +559,9 @@
         return carry
 
     for it in range(pairs):
-        pltpu.make_async_copy(r.firstT.at[it], r.first_rows.at[it], r.first_sem.at[it]).start()
-    lax.fori_loop(0, pairs, patch_pair, 0)
-
-    r.class_grads[:, 0:width] = jnp.sum(r.class_dk[...], axis=1)
-    r.class_grads[:, width:] = jnp.sum(r.class_dv[...], axis=1)
+        one_copy(r.firstT, r.first_rows, r.first_sem, it).start()
+    lax.fori_loop(0, dims.early, one_pair, 0)
+
     if inside:
         sibling(r.crossed_grad, r.returned, r.l_returned).wait()
         sibling(r.grads, r.grads_in, r.l_grads).wait()
@@ -526,114 +570,150 @@
         r.grads_out[...] = r.grads[...] + r.grads_in[...]
         r.shrink_out[...] = r.grads_shrink[...] + r.grads_shrink_in[...]
         peers = pl.ds(0, n_img - 1)
-        wait_all(r.gains.at[peers], r.l_gain.at[0])
-        wait_all(r.region_up.at[peers], r.l_up.at[0])
         wait_all(r.w_all.at[0, peers], r.l_weights.at[0])
         wait_all(r.s_all.at[0, peers], r.l_shrink.at[0])
         wait_all(r.crossed, r.l_crossed.at[0])
     for it in range(pairs):
+        one_copy(r.firstT, r.first_rows, r.first_sem, it).wait()
+    for it in range(dims.early):
         pair_copy(r.tok, r.patch_rows, r.out_sem, it).wait()
-        pltpu.make_async_copy(r.firstT.at[it], r.first_rows.at[it], r.first_sem.at[it]).wait()
-        pltpu.make_async_copy(r.input_grad.at[it], r.grad_rows.at[it], r.grad_sem.at[it]).wait()
-
-
-def class_kernel(dims, *refs):
+        one_copy(r.input_grad, r.grad_rows, r.grad_sem, it).wait()
+    for k, (turned, target) in enumerate(turns):
+        pltpu.make_async_copy(turned, target, r.turn_sem.at[k]).wait()
+
+
+def finish_kernel(dims, *refs):
     r = SimpleNamespace(**dict(zip(dims.names, refs, strict=True)))
-    width = dims.width
-    rows, patches = dims.images, dims.patches
+    width, hidden = dims.width, dims.hidden
+    rows, patches, early = dims.images, dims.patches, dims.early
     pairs, lanes = rows // 2, 2 * patches
-    it = pl.program_id(0)
+    late = pairs - early
+
+    loads = []
+    for k, name in enumerate(dims.staged):
+        load = pltpu.make_async_copy(getattr(r, name), getattr(r, name + BESIDE), r.load_sem.at[k])
+        setattr(r, name, getattr(r, name + BESIDE))
+        loads.append(load)
+    last = pl.ds(2 * early, 2 * late)
+    tok_in = pltpu.make_async_copy(r.tokens.at[last], r.tok, r.late_sem.at[0])
+    cot_in = pltpu.make_async_copy(r.cotangent.at[last], r.cot, r.late_sem.at[1])
+    ready = pl.ds(0, 2 * early)
+    rows_in = pltpu.make_async_copy(r.patch_rows.at[ready], r.ready, r.late_sem.at[2])
+    rows_out = pltpu.make_async_copy(r.ready, r.patch_output.at[ready], r.late_sem.at[4])
+    firsts = [one_copy(r.first_rows, r.firstT, r.first_sem, it) for it in range(pairs)]
+    earlier = [one_copy(r.grad_rows, r.input_grad, r.grad_sem, it) for it in range(early)]
+    bounds = (0,) + dims.bounds
+    stages = [loads[a:b] for a, b in zip(bounds, bounds[1:])]
+    stages[0] = firsts[early:] + [tok_in] + stages[0]
+    stages[2] = [cot_in] + stages[2]
+    stages[3] = stages[3] + firsts[:early] + earlier + [rows_in]
+    for stage in stages:
+        for load in stage:
+            load.start()
+
+    def ready(stage):
+        for load in stages[stage]:
+            load.wait()
+
+    ready(0)
     gain_row = wide_row(r.vectors[...], 0, width // 128)
     regain_row = wide_row(r.vectors[...], width // 128, width // 128)
-
-    @pl.when(it == 0)
-    def _():
-        r.gainT[...] = column(gain_row, lanes)
-        r.ungainT[...] = 1.0 / r.gainT[...]
-        upstream = r.class_up[...]
-        middle = r.class_middle[...]
-        unit, _, inverse = standardize(middle, 1)
-        hidden_low = (nt(upstream, r.frozen_shrink[...]) * r.class_slope[...]).astype(BF16)
-        second_grad = nt(hidden_low, r.frozen_expand[...])
-        middle_grad = upstream.astype(F32) + norm_back(second_grad * regain_row, unit, inverse, 1)
-        r.middle_grad[...] = middle_grad
-        low = nt(middle_grad.astype(BF16), r.frozen_merge[...]).astype(BF16).astype(F32)
-        r.class_low[...] = low
-        low_map = nt(spread(low).astype(BF16), r.frozen_triple[:, 2 * width :])
-        r.low_map[...] = low_map.reshape(rows, HEADS8, width)
-        total = jnp.sum(spread(low * r.class_context[...]), axis=1, keepdims=True)
-        r.class_total[...] = jnp.broadcast_to(total, (rows * HEADS8, 128)).reshape(
-            rows, HEADS8, 128
-        )
-
-    first = r.first_rows[0]
-    maps = jnp.concatenate([r.low_map[2 * it + b] for b in range(2)], axis=0)
-    probs_grads = nn(maps.astype(BF16), first)
-    corrections = []
-    for b in range(2):
-        image = 2 * it + b
-        own_first = first[:, b * patches : (b + 1) * patches]
-        part = probs_grads[b * HEADS8 : (b + 1) * HEADS8, b * patches : (b + 1) * patches]
-        weights = r.class_probs[b]
-        score_grad = weights * (part - r.class_total[image][:, 0:1])
-        r.mixed[image] = nt(score_grad.astype(BF16), own_first)
-        left = jnp.concatenate([r.query_map[b], r.low_map[image]], axis=0)
-        right = jnp.concatenate([score_grad * LN2, weights], axis=0)
-        corrections.append(tn(left.astype(BF16), right.astype(BF16)))
-    correction = jnp.concatenate(corrections, axis=1)
-    inverse = r.stat[0, 1:2, :]
-    scaled = correction * r.gainT[...]
-    firsts = first.astype(F32)
-    along = mean(correction * firsts, 0)
-    back = inverse * (scaled - mean(scaled, 0) - firsts * r.ungainT[...] * along)
-    result = r.grad_rows[0].astype(F32) + back
-    for b in range(2):
-        r.patch_gradient[b] = result[:, b * patches : (b + 1) * patches].astype(BF16).T
-    r.patch_output[...] = r.patch_rows[...]
-
-    @pl.when(it == pairs - 1)
-    def _():
-        low = r.class_low[...]
-        packed = r.class_packed[...]
-        tall_low = spread(low)
-        total = r.class_total[...].reshape(rows * HEADS8, 128)[:, 0:1]
-        self_prob = r.self_prob[...].reshape(rows * HEADS8, 128)[:, 0:1]
-        tall_q = spread(packed[:, 0:width])
-        tall_v = spread(packed[:, 2 * width :])
-        self_grad = self_prob * (jnp.sum(tall_low * tall_v, axis=1, keepdims=True) - total)
-        unit, _, inverse = standardize(r.class_tokens[...].astype(F32), 1)
-        first = (unit * gain_row).astype(BF16).astype(F32)
-        firsts = jnp.broadcast_to(first[:, None, :], (rows, HEADS8, width))
-        mixed = r.mixed[...].reshape(rows * HEADS8, width)
-        mixed = mixed + self_grad * firsts.reshape(rows * HEADS8, width)
-        triple = r.frozen_triple
-        query_grad = gather_heads(nn(mixed.astype(BF16), triple[:, width : 2 * width]))
-        key_grad = jnp.sum((tall_q * self_grad).reshape(rows, HEADS8, width), axis=1)
-        value_grad = jnp.sum((tall_low * self_prob).reshape(rows, HEADS8, width), axis=1)
-        packed_grad = jnp.concatenate(
-            [
-                query_grad * HD ** (-0.5),
-                r.class_grads[:, 0:width] + key_grad * HD ** (-0.5),
-                r.class_grads[:, width:] + value_grad,
-            ],
-            axis=1,
-        ).astype(BF16)
-        first_grad = nt(packed_grad, triple[...])
-        back = norm_back(first_grad * gain_row, unit, inverse, 1)
-        r.class_gradient[...] = (r.middle_grad[...] + back).astype(BF16)
-        if dims.inside:
-            wide = width * 4 + dims.hidden
-            r.region_output[...] = r.region_out[...]
-            r.triple_gradient[...] = r.grads_out[:, 0 : 3 * width]
-            r.merge_gradient[...] = r.grads_out[:, 3 * width : 4 * width]
-            r.expand_gradient[...] = r.grads_out[:, 4 * width : wide]
-            r.shrink_gradient[...] = r.shrink_out[...]
-            shard = r.grads_out.shape[0]
-            blank = jnp.zeros((128 - shard, 128), F32)
-            for k, target in enumerate((r.first_gradient, r.second_gradient)):
-                columns = r.grads_out[:, wide + 128 * k : wide + 128 * (k + 1)]
-                columns = jnp.concatenate([columns, blank], axis=0).T
-                target[...] = columns[0:1, 0:shard]
+    r.gainT[...] = column(gain_row, lanes)
+    r.regainT[...] = column(regain_row, lanes)
+    packed = r.class_packed[...]
+    tall_k = spread(packed[:, width : 2 * width])
+    tall_v = spread(packed[:, 2 * width :])
+    r.class_k[...] = tall_k.reshape(rows, HEADS8, width)
+    r.class_v[...] = tall_v.reshape(rows, HEADS8, width)
+    for it in range(early, pairs):
+        first_one = it == early
+        patch_pair(r, dims, it, it - early, lambda k: ready(k) if first_one and k else None)
+    ready(3)
+    out = pltpu.make_async_copy(r.tok, r.patch_output.at[last], r.late_sem.at[3])
+    out.start()
+    rows_out.start()
+
+    upstream = r.class_up[...]
+    middle = r.class_middle[...]
+    unit, _, inverse = standardize(middle, 1)
+    hidden_low = (nt(upstream, r.frozen_shrink[...]) * r.class_slope[...]).astype(BF16)
+    second_grad = nt(hidden_low, r.frozen_expand[...])
+    middle_grad = upstream.astype(F32) + norm_back(second_grad * regain_row, unit, inverse, 1)
+    low = nt(middle_grad.astype(BF16), r.frozen_merge[...]).astype(BF16).astype(F32)
+    tall_low = spread(low)
+    low_map = nt(tall_low.astype(BF16), r.frozen_triple[:, 2 * width :])
+    r.low_map[...] = low_map.reshape(rows, HEADS8, width)
+    total = jnp.sum(spread(low * r.class_context[...]), axis=1, keepdims=True)
+    r.class_total[...] = jnp.broadcast_to(total, (rows * HEADS8, 128)).reshape(rows, HEADS8, 128)
+    r.ungainT[...] = 1.0 / r.gainT[:, 0:patches]
+
+    def correct(it, carry):
+        first = r.firstT[it]
+        inverse = r.stat[it, 1:2, :]
+        left, right, along = [], [], []
+        maps = jnp.concatenate([r.low_map[2 * it + b] for b in range(2)], axis=0)
+        probs_grads = nn(maps.astype(BF16), first)
+        for b in range(2):
+            image = 2 * it + b
+            span = slice(b * patches, (b + 1) * patches)
+            part = probs_grads[b * HEADS8 : (b + 1) * HEADS8, span]
+            weights = r.class_probs[image]
+            score_grad = weights * (part - r.class_total[image][:, 0:1])
+            r.mixed[image] = nt(score_grad.astype(BF16), first[:, span])
+            toward = jnp.concatenate([r.query_map[image], r.low_map[image]], axis=0) * gain_row
+            left.append((toward - mean(toward, 1)).astype(BF16))
+            scaled = jnp.concatenate([score_grad * LN2, weights], axis=0) * inverse[:, span]
+            right.append(scaled.astype(BF16))
+            scores = jnp.concatenate([r.class_scores[image], part], axis=0)
+            along.append(jnp.sum(scaled * scores, axis=0, keepdims=True) * (1.0 / width))
+        for b in range(2):
+            span = slice(b * patches, (b + 1) * patches)
+            back = tn(left[b], right[b]) - first[:, span].astype(F32) * (r.ungainT[...] * along[b])
+            result = r.input_grad[it, :, span].astype(F32) + back
+            r.result[2 * it + b] = result.astype(BF16).T
+        pair_copy(r.result, r.patch_gradient, r.back_sem, it).start()
+        return carry
+
+    lax.fori_loop(0, pairs, correct, 0, unroll=2)
+
+    self_prob = r.self_prob[...].reshape(rows * HEADS8, 128)[:, 0:1]
+    tall_q = spread(packed[:, 0:width])
+    self_grad = self_prob * (jnp.sum(tall_low * tall_v, axis=1, keepdims=True) - total)
+    unit, _, inverse = standardize(r.class_tokens[...].astype(F32), 1)
+    first = (unit * gain_row).astype(BF16).astype(F32)
+    tall_first = jnp.broadcast_to(first[:, None, :], (rows, HEADS8, width))
+    mixed = r.mixed[...].reshape(rows * HEADS8, width)
+    mixed = mixed + self_grad * tall_first.reshape(rows * HEADS8, width)
+    triple = r.frozen_triple
+    query_grad = gather_heads(nn(mixed.astype(BF16), triple[:, width : 2 * width]))
+    key_grad = r.class_dk[...] + (tall_q * (self_grad * HD ** (-0.5))).reshape(
+        rows, HEADS8, width
+    )
+    value_grad = r.class_dv[...] + (tall_low * self_prob).reshape(rows, HEADS8, width)
+    packed_grad = jnp.concatenate(
+        [query_grad * HD ** (-0.5), jnp.sum(key_grad, axis=1), jnp.sum(value_grad, axis=1)],
+        axis=1,
+    ).astype(BF16)
+    first_grad = nt(packed_grad, triple[...])
+    back = norm_back(first_grad * gain_row, unit, inverse, 1)
+    r.class_gradient[...] = (middle_grad + back).astype(BF16)
+    if dims.inside:
+        wide = width * 4 + hidden
+        r.region_output[...] = r.region_out[...]
+        r.triple_gradient[...] = r.grads_out[:, 0 : 3 * width]
+        r.merge_gradient[...] = r.grads_out[:, 3 * width : 4 * width]
+        r.expand_gradient[...] = r.grads_out[:, 4 * width : wide]
+        r.shrink_gradient[...] = r.shrink_out[...]
+        shard = r.grads_out.shape[0]
+        blank = jnp.zeros((128 - shard, 128), F32)
+        for k, target in enumerate((r.first_gradient, r.second_gradient)):
+            columns = r.grads_out[:, wide + 128 * k : wide + 128 * (k + 1)]
+            columns = jnp.concatenate([columns, blank], axis=0).T
+            target[...] = columns[0:1, 0:shard]
+    rows_out.wait()
+    out.wait()
+    for it in range(pairs):
+        pair_copy(r.result, r.patch_gradient, r.back_sem, it).wait()
 
 
 def normalize(values, scaling):
@@ -857,7 +937,7 @@
     images = micros * per
     shard, shard_ff = width // n_img, hidden // n_img
     lanes, pairs, keys, heads = 2 * patches, images // 2, n_img * images, width // HD
-    inside = keys == patches and shard % 8 == 0 and shard <= PAD
+    inside = keys == patches and shard == PAD - 8 and images == 16 and width == 384
 
     vectors = [frozen_gain, frozen_regain]
     if inside:
@@ -895,6 +975,10 @@
         patch_rows=shape((images, patches, width), BF16),
         first_rows=shape((pairs, width, lanes), BF16),
         grad_rows=shape((pairs, width, lanes), BF16),
+        triple_turned=shape((3 * width, width), BF16),
+        merge_turned=shape((width, width), BF16),
+        expand_turned=shape((hidden, width), BF16),
+        shrink_turned=shape((width, hidden), BF16),
     )
     small = dict(
         stat=shape((pairs, 8, lanes), F32),
@@ -904,8 +988,10 @@
         class_slope=shape((images, hidden), F32),
         query_map=shape((images, HEADS8, width), F32),
         class_probs=shape((images, HEADS8, patches), F32),
+        class_scores=shape((images, HEADS8, patches), F32),
         self_prob=shape((images, HEADS8, 128), F32),
-        class_grads=shape((images, 2 * width), F32),
+        class_dk=shape((images, HEADS8, width), F32),
+        class_dv=shape((images, HEADS8, width), F32),
     )
     if inside:
         small |= dict(
@@ -921,15 +1007,7 @@
 
     v = pltpu.VMEM
     dma = pltpu.SemaphoreType.DMA
-    scratch = dict(
-        tok=v((images, patches, width), BF16),
-        cot=v((images, patches, width), BF16),
-        firstT=v((pairs, width, lanes), BF16),
-        input_grad=v((pairs, width, lanes), BF16),
-        tripleT=v((3 * width, width), BF16),
-        mergeT=v((width, width), BF16),
-        expandT=v((hidden, width), BF16),
-        shrinkT=v((width, hidden), BF16),
+    working = dict(
         gainT=v((width, lanes), F32),
         regainT=v((width, lanes), F32),
         qkv=v((3 * width, lanes), BF16),
@@ -943,16 +1021,27 @@
         low_grad=v((width, lanes), BF16),
         class_k=v((images, HEADS8, width), F32),
         class_v=v((images, HEADS8, width), F32),
-        class_dk=v((images, HEADS8, width), F32),
-        class_dv=v((images, HEADS8, width), F32),
+        mixed=v((images, HEADS8, width), F32),
+        firstT=v((pairs, width, lanes), BF16),
+        input_grad=v((pairs, width, lanes), BF16),
+        first_sem=dma((pairs,)),
+        grad_sem=dma((pairs,)),
+    )
+    turned = dict(
+        tripleT=v((3 * width, width), BF16),
+        mergeT=v((width, width), BF16),
+        expandT=v((hidden, width), BF16),
+        shrinkT=v((width, hidden), BF16),
+    )
+    scratch = working | turned | dict(
+        tok=v((images, patches, width), BF16),
+        cot=v((images, patches, width), BF16),
         class_first=v((images, HEADS8, width), F32),
-        mixed=v((images, HEADS8, width), F32),
         self_score=v((images, HEADS8, 128), F32),
         tok_sem=dma((pairs,)),
         cot_sem=dma((pairs,)),
         out_sem=dma((pairs,)),
-        first_sem=dma((pairs,)),
-        grad_sem=dma((pairs,)),
+        turn_sem=dma((len(turned),)),
     )
     if inside:
         deep = PAD * n_img
@@ -961,9 +1050,6 @@
             crossed=v((n_img, images, width), BF16),
             crossed_grad=v((images, width), BF16),
             returned=v((images, width), BF16),
-            region_up=v((n_img, images, width), BF16),
-            gain_own=v((2 * shard, 128), F32),
-            gains=v((n_img, 2 * shard, 128), F32),
             w_own=v((2, PAD, 4 * width), BF16),
             w_all=v((2, n_img, PAD, 4 * width), BF16),
             s_own=v((2, shard_ff // 2, width), BF16),
@@ -979,8 +1065,6 @@
             grads_in=v((shard, columns), F32),
             grads_shrink=v((shard_ff, width), F32),
             grads_shrink_in=v((shard_ff, width), F32),
-            l_gain=dma((2,)),
-            l_up=dma((2,)),
             l_weights=dma((2,)),
             l_shrink=dma((2,)),
             l_forward=dma((2,)),
@@ -991,7 +1075,13 @@
             l_grads_shrink=dma((2,)),
         )
     sizes = dict(
-        n_img=n_img, width=width, hidden=hidden, images=images, patches=patches, inside=inside
+        n_img=n_img,
+        width=width,
+        hidden=hidden,
+        images=images,
+        patches=patches,
+        inside=inside,
+        early=pairs - LATE,
     )
     limit = dict(vmem_limit_bytes=60 * 1024 * 1024)
     remote = dict(collective_id=0, has_side_effects=True) if inside else {}
@@ -1016,31 +1106,40 @@
         )
         done |= dict(class_up=class_up.reshape(images, width))
 
-    def step(*block):
-        return pl.BlockSpec(block, lambda it: (it,) + (0,) * (len(block) - 1))
-
-    specs = dict(
-        patch_rows=step(2, patches, width),
-        first_rows=step(1, width, lanes),
-        grad_rows=step(1, width, lanes),
-        stat=step(1, 8, lanes),
-        query_map=step(2, HEADS8, width),
-        class_probs=step(2, HEADS8, patches),
-    )
-    inputs = done | dict(
-        class_tokens=class_rows,
-        vectors=vectors,
-        frozen_triple=frozen_triple,
-        frozen_merge=frozen_merge,
-        frozen_expand=frozen_expand,
-        frozen_shrink=frozen_shrink,
-    )
+    streamed = [done.pop(name) for name in large]
+    done = SimpleNamespace(**done)
+    tripleT, mergeT, expandT, shrinkT = streamed[-len(turned) :]
+    stages = (
+        dict(vectors=vectors, class_packed=done.class_packed, stat=done.stat, tripleT=tripleT),
+        dict(mergeT=mergeT, expandT=expandT, shrinkT=shrinkT),
+        dict(
+            frozen_shrink=frozen_shrink,
+            frozen_expand=frozen_expand,
+            frozen_merge=frozen_merge,
+            frozen_triple=frozen_triple,
+            class_dk=done.class_dk,
+            class_dv=done.class_dv,
+        ),
+        dict(class_tokens=class_rows) | vars(done),
+    )
+    staged, bounds = {}, ()
+    for stage in stages:
+        staged |= {name: a for name, a in stage.items() if name not in staged}
+        bounds += (len(staged),)
+    inputs = dict(
+        tokens=patch_tokens.reshape(images, patches, width),
+        cotangent=patch_cotangent.reshape(images, patches, width),
+        patch_rows=streamed[0],
+        first_rows=streamed[1],
+        grad_rows=streamed[2],
+    )
+    inputs |= staged
     outputs = dict(
         patch_output=shape((images, patches, width), BF16),
         patch_gradient=shape((images, patches, width), BF16),
         class_gradient=shape((images, width), BF16),
     )
-    out_specs = [step(2, patches, width)] * 2 + [vmem]
+    out_specs = [hbm] * 2 + [vmem]
     if inside:
         ready = dict(
             region_output=shape((images, width), BF16),
@@ -1053,21 +1152,25 @@
         )
         outputs |= ready
         out_specs += [vmem] * len(ready)
-    scratch = dict(
-        gainT=v((width, lanes), F32),
-        ungainT=v((width, lanes), F32),
-        middle_grad=v((images, width), F32),
-        class_low=v((images, width), F32),
+    scratch = working | dict(
+        tok=v((2 * LATE, patches, width), BF16),
+        cot=v((2 * LATE, patches, width), BF16),
+        result=v((images, patches, width), BF16),
+        ungainT=v((width, patches), F32),
         low_map=v((images, HEADS8, width), F32),
         class_total=v((images, HEADS8, 128), F32),
-        mixed=v((images, HEADS8, width), F32),
-    )
+        load_sem=dma((len(staged),)),
+        ready=v((images - 2 * LATE, patches, width), BF16),
+        late_sem=dma((5,)),
+        back_sem=dma((pairs,)),
+    )
+    scratch |= {name + BESIDE: v(a.shape, a.dtype) for name, a in staged.items()}
     names = list(inputs) + list(outputs) + list(scratch)
+    sizes |= dict(names=names, staged=list(staged), bounds=bounds)
     results = pl.pallas_call(
-        functools.partial(class_kernel, SimpleNamespace(names=names, **sizes)),
-        grid=(pairs,),
+        functools.partial(finish_kernel, SimpleNamespace(**sizes)),
         out_shape=list(outputs.values()),
-        in_specs=[specs.get(name, vmem) for name in inputs],
+        in_specs=[hbm] * len(inputs),
         out_specs=out_specs,
         scratch_shapes=list(scratch.values()),
         compiler_params=pltpu.CompilerParams(**limit),

time: 128 us -> 115 us (0.90)
  Pallas kernels: 126 us -> 112 us
    pallas_call x1, Pallas kernels: 111 us -> 91 us  [local(): pl.pallas_call(functools.partial(patch_kernel, SimpleNamespace(names=name...]
    pallas_call x1, Pallas kernels: 15.4 us -> 21.3 us  [local(): pl.pallas_call(functools.partial(finish_kernel, SimpleNamespace(**sizes))...]
where the time goes in v2:
time: 115 us; the launch traced here: 114 us
  Pallas kernels  112 us (97%)
  other arithmetic  1.33 us (1%)
    pallas_call x1, Pallas kernels, local(): pl.pallas_call(functools.partial(patch_kernel, SimpleNamespace(names=name...  91 us
    pallas_call x1, Pallas kernels, local(): pl.pallas_call(functools.partial(finish_kernel, SimpleNamespace(**sizes))...  21.3 us

profile of v2, /device:TPU:0, one launch (start us, length us, event | category | flops | bytes accessed | tf_op | source)
XLA Modules:
  0.0 114.4 jit_solution(5432769995921246334)
XLA Ops:
  0.6 1.3 %fusion.6.refs_3_.refs_5_ = f32[8,128]{1,0:T(8,128)} fusion(bf16[24]{0:T(256)(128)(2,1)} %param.29, bf16[24]{0:T(256)(128)(2,1)} %param.26, bf16[384]{0:T(512)(128)(2,1)} %param.23, bf16[384]{0:T(512)(128)(2,1)} %param.20), kind=kLoop, calls=%fused_computation.9 | loop fusion | flops 15360 | bytes 5728 | tf_op jit(solution)/shard_map/convert_element_type | solution.py:946
  2.0 91.0 %shard_map.240 = (bf16[16,256,384]{2,1,0:T(8,128)(2,1)}, bf16[8,384,512]{2,1,0:T(8,128)(2,1)}, bf16[8,384,512]{2,1,0:T(8,128)(2,1)}, bf16[1152,384]{1,0:T(8,128)...) custom-call(bf16[16,256,384]{2,1,0:T(8,128)(2,1)} %bitcast.15, ...), custom_call_target="tpu_custom_call" | custom-call | tf_op jit(solution)/shard_map/pallas_call | solution.py:1089
  93.0 21.3 %shard_map.241 = (bf16[16,256,384]{2,1,0:T(8,128)(2,1)}, bf16[16,256,384]{2,1,0:T(8,128)(2,1)}, bf16[16,384]{1,0:T(8,128)(2,1)}, bf16[16,384]{1,0:T(8,128)(2,1)}...) custom-call(bf16[16,256,384]{2,1,0:T(8,128)(2,1)} %bitcast.16, ...), custom_call_target="tpu_custom_call" | custom-call | tf_op jit(solution)/shard_map/pallas_call | solution.py:1170

commit v3 on v2

--- a/solution.py
+++ b/solution.py
@@ -17,6 +17,7 @@
 LN2 = 0.6931471805599453
 ROOT_HALF = 0.7071067811865476
 DENSITY = 0.3989422804014327
+LOG2_DENSITY = -1.3257480647361593
 F32 = jnp.float32
 BF16 = jnp.bfloat16
 MESH = pl.DeviceIdType.MESH
@@ -64,6 +65,13 @@
     return hidden * upto, upto + hidden * (bell * DENSITY)
 
 
+def gelu_pair_low(half):
+    twice = (1.0 + lax.erf(half * (2.0 * ROOT_HALF))).astype(BF16)
+    bell = jnp.exp2(half * half * (-2.0 * LOG2E) + (LOG2_DENSITY + 2.0)).astype(BF16)
+    low = half.astype(BF16)
+    return low * twice, twice + low * bell
+
+
 def own_heads(rows, width):
     shape = (rows * HEADS8, width)
     lane = lax.broadcasted_iota(jnp.int32, shape, 1) // HD
@@ -80,10 +88,6 @@
     tall, width = values.shape
     kept = jnp.where(own_heads(tall // HEADS8, width), values, 0.0)
     return jnp.sum(kept.reshape(tall // HEADS8, HEADS8, width), axis=1)
-
-
-def wide_row(vectors, first, count):
-    return jnp.concatenate([vectors[k : k + 1, :] for k in range(first, first + count)], axis=1)
 
 
 def column(row, lanes):
@@ -112,18 +116,21 @@
     return jnp.concatenate([values[PAD * j : PAD * j + shard] for j in range(n)], axis=0)
 
 
-def patch_pair(r, dims, it, slot, ready=lambda stage: None):
+def project(r, dims, it):
+    width = dims.width
+    first = r.firstT[it]
+    queries = nn(r.tripleT[0:width, :], first) * (LOG2E * HD ** (-0.5))
+    r.qkv[0:width, :] = queries.astype(BF16)
+    r.qkv[width:, :] = nn(r.tripleT[width:, :], first).astype(BF16)
+
+
+def patch_pair(r, dims, it, slot, following, ready=lambda stage: None):
     width, hidden, patches = dims.width, dims.hidden, dims.patches
     heads = width // HD
     block_head = own_heads(1, width)
     span = [slice(b * patches, (b + 1) * patches) for b in range(2)]
     qkv, ctx, probs = r.qkv, r.ctx, r.probs
     values = jnp.concatenate([r.tok[2 * slot + b].T for b in range(2)], axis=1).astype(F32)
-    ready(0)
-    first = r.firstT[it]
-    queries = nn(r.tripleT[0:width, :], first) * (LOG2E * HD ** (-0.5))
-    qkv[0:width, :] = queries.astype(BF16)
-    qkv[width:, :] = nn(r.tripleT[width:, :], first).astype(BF16)
     order = [(b, h) for h in range(heads) for b in range(2)]
     key_rows = [r.class_k[2 * it + b].astype(BF16) for b in range(2)]
     value_rows = [r.class_v[2 * it + b].astype(BF16) for b in range(2)]
@@ -159,28 +166,38 @@
             mix = mixes[2 * h + b] + from_class[at]
             ctx[at, span[b]] = (mix * shares[2 * h + b]).astype(BF16)
     ready(1)
-    middle = values + nn(r.mergeT[...], ctx[...])
+    merged = nn(r.mergeT[...], ctx[...])
+    upstream = jnp.concatenate([r.cot[2 * slot + b].T for b in range(2)], axis=1)
+    half_upstream = upstream * BF16(0.5)
+    chunks = [slice(c, c + width) for c in range(0, hidden, width)]
+
+    def active_grad(at):
+        return nn(r.frozen_shrink[at, :], half_upstream).astype(BF16)
+
+    ahead = len(chunks) // 2
+    active_grads = [active_grad(at) for at in chunks[:ahead]]
+    middle = values + merged
     unit_b, _, inverse_b = standardize(middle, 0)
     second = (unit_b * r.regainT[...]).astype(BF16)
-    chunk = width
-    for c in range(0, hidden, chunk):
-        at = slice(c, c + chunk)
-        active, slope = gelu_pair(nn(r.expandT[at, :], second))
+    coming = nn(r.expandT[chunks[0], :], second)
+    for k, at in enumerate(chunks):
+        current = coming
+        if k + 1 < len(chunks):
+            coming = nn(r.expandT[chunks[k + 1], :], second)
+        if ahead + k < len(chunks):
+            active_grads.append(active_grad(chunks[ahead + k]))
+        active, slope = gelu_pair_low(current)
         r.active[at, :] = active.astype(BF16)
-        r.slope[at, :] = slope.astype(BF16)
-    result = middle + nn(r.shrinkT[...], r.active[...])
+        r.slope[at, :] = active_grads[k] * slope.astype(BF16)
+    ready(2)
+    second_grad = nn(r.frozen_expand[...], r.slope[...])
+    shrunk = nn(r.shrinkT[...], r.active[...])
+    middle_grad = upstream.astype(F32) + norm_back(
+        second_grad * r.regainT[...], unit_b, inverse_b, 0
+    )
+    result = middle + shrunk
     for b in range(2):
         r.tok[2 * slot + b] = result[:, span[b]].astype(BF16).T
-    ready(2)
-    upstream = jnp.concatenate([r.cot[2 * slot + b].T for b in range(2)], axis=1)
-    for c in range(0, hidden, chunk):
-        at = slice(c, c + chunk)
-        active_grad = nn(r.frozen_shrink[at, :], upstream)
-        r.active[at, :] = active_grad.astype(BF16) * r.slope[at, :]
-    second_grad = nn(r.frozen_expand[...], r.active[...])
-    middle_grad = upstream.astype(F32) + norm_back(
-        second_grad * r.regainT[...], unit_b, inverse_b, 0
-    )
     context_grad = nn(r.frozen_merge[...], middle_grad.astype(BF16))
     low_grad, packed_grad = r.low_grad, r.packed_grad
     totals, from_class = [[], []], []
@@ -230,6 +247,8 @@
             key_and_query(turn - 1, score_grads.pop(turn - 1))
     key_and_query(len(order) - 1, score_grads.pop(len(order) - 1))
     first_grad = nn(r.frozen_triple[...], packed_grad[...])
+    if following is not None:
+        project(r, dims, following)
     centre, inverse = r.stat[it, 0:1, :], r.stat[it, 1:2, :]
     unit = (values - centre) * inverse
     back = norm_back(first_grad * r.gainT[...], unit, inverse, 0)
@@ -311,12 +330,11 @@
     for it in range(dims.early):
         pair_copy(r.cotangent, r.cot, r.cot_sem, it).start()
 
-    vectors = r.vectors[...]
-    gain_row = wide_row(vectors, 0, width // 128)
-    regain_row = wide_row(vectors, width // 128, width // 128)
+    gain_row = r.frozen_gain[...].astype(F32).reshape(1, width)
+    regain_row = r.frozen_regain[...].astype(F32).reshape(1, width)
     r.tripleT[...] = r.frozen_triple[...].T
     r.mergeT[...] = r.frozen_merge[...].T
-    r.expandT[...] = r.frozen_expand[...].T
+    r.expandT[...] = r.frozen_expand[...].T * BF16(0.5)
     r.shrinkT[...] = r.frozen_shrink[...].T
     turns = (
         (r.tripleT, r.triple_turned),
@@ -332,9 +350,11 @@
     if inside:
         upstream = r.region_cotangent[...].astype(F32)
         fill = [upstream[8 * k : 8 * k + 8] for k in range(rows // 8)]
+        r.shard_gains[...] = jnp.zeros_like(r.shard_gains)
+        r.shard_gains[0:1, 0:shard] = r.gain_first[...].astype(F32).reshape(1, shard)
+        r.shard_gains[1:2, 0:shard] = r.gain_second[...].astype(F32).reshape(1, shard)
         for k in range(2):
-            row = vectors[2 * width // 128 + k : 2 * width // 128 + k + 1, :]
-            tall = column(row, 128)
+            tall = column(r.shard_gains[k : k + 1, :], 128)
             fill += [tall[at : at + 8] for at in range(0, shard, 8)]
         fill = jnp.concatenate(fill, axis=1)
         triple = r.weight_triple[...].astype(F32)
@@ -464,18 +484,21 @@
         packed = tn(w_triple, r.region_first[...])
         qkv[0:width, 0:keys] = (packed[0:width] * (LOG2E * HD ** (-0.5))).astype(BF16)
         qkv[width:, 0:keys] = packed[width:].astype(BF16)
-        mixes = []
+
+        def part(which, h):
+            return qkv[which * width + HD * h : which * width + HD * (h + 1), 0:keys]
+
+        mixes, scores = [], [tn(part(1, 0), part(0, 0))]
         for h in range(heads):
-            q = qkv[HD * h : HD * (h + 1), 0:keys]
-            k = qkv[width + HD * h : width + HD * (h + 1), 0:keys]
-            v = qkv[2 * width + HD * h : 2 * width + HD * (h + 1), 0:keys]
-            scores = tn(k, q) + bias
-            weights = jnp.exp2(scores - jnp.max(scores, axis=0, keepdims=True))
-            share = 1.0 / jnp.sum(weights, axis=0, keepdims=True)
-            low = weights.astype(BF16)
-            probs[h] = low
-            r.shares[0, h : h + 1, :] = share
-            mixes.append(nn(v, low) * share)
+            if h + 1 < heads:
+                scores.append(tn(part(1, h + 1), part(0, h + 1)))
+            biased = scores[h] + bias
+            weights = jnp.exp2(biased - jnp.max(biased, axis=0, keepdims=True))
+            r.shares[0, h : h + 1, :] = 1.0 / jnp.sum(weights, axis=0, keepdims=True)
+            probs[h] = weights.astype(BF16)
+            if h:
+                mixes.append(nn(part(2, h - 1), probs[h - 1]) * r.shares[0, h - 1 : h, :])
+        mixes.append(nn(part(2, heads - 1), probs[heads - 1]) * r.shares[0, heads - 1 : heads, :])
         context = jnp.concatenate(mixes, axis=0)
         r.region_context[...] = padded(context, shard, n_img).astype(BF16)
         middle = values + tn(w_merge, r.region_context[...])
@@ -501,23 +524,32 @@
         middle_low = middle_grad.astype(BF16)
         context_grad = trimmed(nn(w_merge, middle_low), shard, n_img)
         packed_grad = r.packed_grad
+        lows, totals = [], []
         for h in range(heads):
             at = slice(HD * h, HD * (h + 1))
-            q = qkv[at, 0:keys]
-            k = qkv[width + HD * h : width + HD * (h + 1), 0:keys]
-            v = qkv[2 * width + HD * h : 2 * width + HD * (h + 1), 0:keys]
-            part = context_grad[at] * r.shares[0, h : h + 1, :]
-            total = jnp.sum(part * context[at], axis=0, keepdims=True)
-            low = part.astype(BF16)
-            weights = probs[h]
-            score_grad = (weights.astype(F32) * (tn(v, low) - total)).astype(BF16)
-            packed_grad[at, 0:keys] = (nn(k, score_grad) * HD ** (-0.5)).astype(BF16)
-            packed_grad[width + HD * h : width + HD * (h + 1), 0:keys] = (
-                nt(q, score_grad) * LN2
-            ).astype(BF16)
-            packed_grad[2 * width + HD * h : 2 * width + HD * (h + 1), 0:keys] = (
-                nt(low, weights).astype(BF16)
+            low = context_grad[at] * r.shares[0, h : h + 1, :]
+            totals.append(jnp.sum(low * context[at], axis=0, keepdims=True))
+            lows.append(low.astype(BF16))
+
+        def put(which, h, grad):
+            packed_grad[which * width + HD * h : which * width + HD * (h + 1), 0:keys] = (
+                grad.astype(BF16)
             )
+
+        def key_and_query(h, score_grad):
+            put(1, h, nt(part(0, h), score_grad) * LN2)
+            put(0, h, nn(part(1, h), score_grad) * HD ** (-0.5))
+
+        grads, score_grads = [tn(part(2, 0), lows[0])], []
+        for h in range(heads):
+            if h + 1 < heads:
+                grads.append(tn(part(2, h + 1), lows[h + 1]))
+            put(2, h, nt(lows[h], probs[h]))
+            score_grad = probs[h].astype(F32) * (grads[h] - totals[h])
+            score_grads.append(score_grad.astype(BF16))
+            if h:
+                key_and_query(h - 1, score_grads[h - 1])
+        key_and_query(heads - 1, score_grads[heads - 1])
         first_grad = trimmed(nn(w_triple, packed_grad[:, 0:keys]), shard, n_img)
         back = norm_back(first_grad * gain, unit, inverse, 0)
         r.region_rows[...] = (middle_grad + back).T
@@ -542,7 +574,7 @@
 
     def one_pair(it, carry):
         pair_copy(r.cotangent, r.cot, r.cot_sem, it).wait()
-        patch_pair(r, dims, it, it)
+        patch_pair(r, dims, it, it, jnp.minimum(it + 1, pairs - 1))
         pair_copy(r.tok, r.patch_rows, r.out_sem, it).start()
         one_copy(r.input_grad, r.grad_rows, r.grad_sem, it).start()
 
@@ -560,6 +592,7 @@
 
     for it in range(pairs):
         one_copy(r.firstT, r.first_rows, r.first_sem, it).start()
+    project(r, dims, 0)
     lax.fori_loop(0, dims.early, one_pair, 0)
 
     if inside:
@@ -605,9 +638,8 @@
     bounds = (0,) + dims.bounds
     stages = [loads[a:b] for a, b in zip(bounds, bounds[1:])]
     stages[0] = firsts[early:] + [tok_in] + stages[0]
-    stages[2] = [cot_in] + stages[2]
-    stages[3] = stages[3] + firsts[:early] + earlier + [rows_in]
-    for stage in stages:
+    stages[1] = [cot_in] + stages[1]
+    for stage in stages + [firsts[:early] + earlier + [rows_in]]:
         for load in stage:
             load.start()
 
@@ -616,8 +648,8 @@
             load.wait()
 
     ready(0)
-    gain_row = wide_row(r.vectors[...], 0, width // 128)
-    regain_row = wide_row(r.vectors[...], width // 128, width // 128)
+    gain_row = r.frozen_gain[...].astype(F32).reshape(1, width)
+    regain_row = r.frozen_regain[...].astype(F32).reshape(1, width)
     r.gainT[...] = column(gain_row, lanes)
     r.regainT[...] = column(regain_row, lanes)
     packed = r.class_packed[...]
@@ -625,13 +657,14 @@
     tall_v = spread(packed[:, 2 * width :])
     r.class_k[...] = tall_k.reshape(rows, HEADS8, width)
     r.class_v[...] = tall_v.reshape(rows, HEADS8, width)
+    project(r, dims, early)
     for it in range(early, pairs):
-        first_one = it == early
-        patch_pair(r, dims, it, it - early, lambda k: ready(k) if first_one and k else None)
+        following = it + 1 if it + 1 < pairs else None
+        wait = ready if it == early else lambda stage: None
+        patch_pair(r, dims, it, it - early, following, wait)
     ready(3)
     out = pltpu.make_async_copy(r.tok, r.patch_output.at[last], r.late_sem.at[3])
     out.start()
-    rows_out.start()
 
     upstream = r.class_up[...]
     middle = r.class_middle[...]
@@ -646,6 +679,9 @@
     total = jnp.sum(spread(low * r.class_context[...]), axis=1, keepdims=True)
     r.class_total[...] = jnp.broadcast_to(total, (rows * HEADS8, 128)).reshape(rows, HEADS8, 128)
     r.ungainT[...] = 1.0 / r.gainT[:, 0:patches]
+    for load in firsts[:early] + earlier + [rows_in]:
+        load.wait()
+    rows_out.start()
 
     def correct(it, carry):
         first = r.firstT[it]
@@ -939,17 +975,13 @@
     lanes, pairs, keys, heads = 2 * patches, images // 2, n_img * images, width // HD
     inside = keys == patches and shard == PAD - 8 and images == 16 and width == 384
 
-    vectors = [frozen_gain, frozen_regain]
-    if inside:
-        vectors += [jnp.pad(g, (0, 128 - shard)) for g in (gain_first, gain_second)]
-    vectors = jnp.concatenate(vectors)
-    vectors = jnp.pad(vectors, (0, 1024 - vectors.shape[0])).astype(F32).reshape(8, 128)
     class_rows = class_tokens.reshape(images, width)
     inputs = dict(
         tokens=patch_tokens.reshape(images, patches, width),
         cotangent=patch_cotangent.reshape(images, patches, width),
         class_tokens=class_rows,
-        vectors=vectors,
+        frozen_gain=frozen_gain,
+        frozen_regain=frozen_regain,
         frozen_triple=frozen_triple,
         frozen_merge=frozen_merge,
         frozen_expand=frozen_expand,
@@ -957,6 +989,8 @@
     )
     if inside:
         inputs |= dict(
+            gain_first=gain_first,
+            gain_second=gain_second,
             region_cotangent=region_cotangent.reshape(images, width),
             region_number=region_number,
             weight_triple=weight_triple,
@@ -1050,6 +1084,7 @@
             crossed=v((n_img, images, width), BF16),
             crossed_grad=v((images, width), BF16),
             returned=v((images, width), BF16),
+            shard_gains=v((8, 128), F32),
             w_own=v((2, PAD, 4 * width), BF16),
             w_all=v((2, n_img, PAD, 4 * width), BF16),
             s_own=v((2, shard_ff // 2, width), BF16),
@@ -1110,10 +1145,10 @@
     done = SimpleNamespace(**done)
     tripleT, mergeT, expandT, shrinkT = streamed[-len(turned) :]
     stages = (
-        dict(vectors=vectors, class_packed=done.class_packed, stat=done.stat, tripleT=tripleT),
-        dict(mergeT=mergeT, expandT=expandT, shrinkT=shrinkT),
+        dict(class_packed=done.class_packed, stat=done.stat, tripleT=tripleT),
+        dict(mergeT=mergeT, frozen_shrink=frozen_shrink, expandT=expandT),
         dict(
-            frozen_shrink=frozen_shrink,
+            shrinkT=shrinkT,
             frozen_expand=frozen_expand,
             frozen_merge=frozen_merge,
             frozen_triple=frozen_triple,
@@ -1134,6 +1169,7 @@
         grad_rows=streamed[2],
     )
     inputs |= staged
+    inputs |= dict(frozen_gain=frozen_gain, frozen_regain=frozen_regain)
     outputs = dict(
         patch_output=shape((images, patches, width), BF16),
         patch_gradient=shape((images, patches, width), BF16),
@@ -1170,7 +1206,7 @@
     results = pl.pallas_call(
         functools.partial(finish_kernel, SimpleNamespace(**sizes)),
         out_shape=list(outputs.values()),
-        in_specs=[hbm] * len(inputs),
+        in_specs=[hbm] * (len(inputs) - 2) + [vmem] * 2,
         out_specs=out_specs,
         scratch_shapes=list(scratch.values()),
         compiler_params=pltpu.CompilerParams(**limit),

time: 115 us -> 110 us (0.957)
  Pallas kernels: 112 us -> 109 us
  other arithmetic: 1.33 us -> 0 us
    pallas_call x1, Pallas kernels: 91 us -> 87.2 us  [local(): pl.pallas_call(functools.partial(patch_kernel, SimpleNamespace(names=name...]
    convert_element_type x1 -> x0, other arithmetic: 1.33 us -> none  [local(): jnp.pad(vectors, (0, 1024 - vectors.shape[0])).astype(F32).reshape(8, 128)]
where the time goes in v3:
time: 110 us; the launch traced here: 109 us
  Pallas kernels  109 us (99%)
    pallas_call x1, Pallas kernels, local(): pl.pallas_call(functools.partial(patch_kernel, SimpleNamespace(names=name...  87.2 us
    pallas_call x1, Pallas kernels, local(): pl.pallas_call(functools.partial(finish_kernel, SimpleNamespace(**sizes))...  21.4 us

profile of v3, /device:TPU:0, one launch (start us, length us, event | category | flops | bytes accessed | tf_op | source)
XLA Modules:
  0.0 109.5 jit_solution(11767943253275060750)
XLA Ops:
  0.6 87.2 %shard_map.240 = (bf16[16,256,384]{2,1,0:T(8,128)(2,1)}, bf16[8,384,512]{2,1,0:T(8,128)(2,1)}, bf16[8,384,512]{2,1,0:T(8,128)(2,1)}, bf16[1152,384]{1,0:T(8,128)...) custom-call(bf16[16,256,384]{2,1,0:T(8,128)(2,1)} %bitcast.10, ...), custom_call_target="tpu_custom_call" | custom-call | tf_op jit(solution)/shard_map/pallas_call | solution.py:1124
  87.9 21.4 %shard_map.241 = (bf16[16,256,384]{2,1,0:T(8,128)(2,1)}, bf16[16,256,384]{2,1,0:T(8,128)(2,1)}, bf16[16,384]{1,0:T(8,128)(2,1)}, bf16[16,384]{1,0:T(8,128)(2,1)}...) custom-call(bf16[16,256,384]{2,1,0:T(8,128)(2,1)} %bitcast.11, ...), custom_call_target="tpu_custom_call" | custom-call | tf_op jit(solution)/shard_map/pallas_call | solution.py:1206

commit v4 on v3

--- a/solution.py
+++ b/solution.py
@@ -387,7 +387,7 @@
         class_first.astype(F32)[:, None, :], (rows, HEADS8, width)
     )
 
-    def class_forward(it, carry):
+    def class_norm(it):
         pair_copy(r.tokens, r.tok, r.tok_sem, it).wait()
         values = jnp.concatenate([r.tok[2 * it + b].T for b in range(2)], axis=1).astype(F32)
         unit, centre, inverse = standardize(values, 0)
@@ -395,30 +395,41 @@
         r.firstT[it] = first
         r.stat[it, 0:1, :] = centre
         r.stat[it, 1:2, :] = inverse
-        maps = jnp.concatenate([r.query_map[2 * it + b] for b in range(2)], axis=0)
-        scores = nn(maps.astype(BF16), first)
-        for b in range(2):
-            part = scores[b * HEADS8 : (b + 1) * HEADS8, b * patches : (b + 1) * patches]
-            r.class_scores[2 * it + b] = part
-            alone = r.self_score[2 * it + b][:, 0:1]
-            top = jnp.maximum(jnp.max(part, axis=1, keepdims=True), alone)
-            weights = jnp.exp2(part - top)
-            weight_alone = jnp.exp2(alone - top)
-            share = 1.0 / (jnp.sum(weights, axis=1, keepdims=True) + weight_alone)
-            weights = weights * share
-            weight_alone = weight_alone * share
-            r.class_probs[2 * it + b] = weights
-            r.self_prob[2 * it + b] = jnp.broadcast_to(weight_alone, (HEADS8, 128))
-            mixed = nt(weights.astype(BF16), first[:, b * patches : (b + 1) * patches])
-            r.mixed[2 * it + b] = mixed + weight_alone * r.class_first[2 * it + b]
+        return first
+
+    def class_forward(step, carry):
+        turns = [2 * step, 2 * step + 1]
+        firsts = [class_norm(it) for it in turns]
+        scores = []
+        for it, first in zip(turns, firsts):
+            maps = jnp.concatenate([r.query_map[2 * it + b] for b in range(2)], axis=0)
+            scores.append(nn(maps.astype(BF16), first))
+        spread_out = []
+        for it, first, score in zip(turns, firsts, scores):
+            for b in range(2):
+                part = score[b * HEADS8 : (b + 1) * HEADS8, b * patches : (b + 1) * patches]
+                r.class_scores[2 * it + b] = part
+                alone = r.self_score[2 * it + b][:, 0:1]
+                top = jnp.maximum(jnp.max(part, axis=1, keepdims=True), alone)
+                weights = jnp.exp2(part - top)
+                weight_alone = jnp.exp2(alone - top)
+                share = 1.0 / (jnp.sum(weights, axis=1, keepdims=True) + weight_alone)
+                weights = weights * share
+                weight_alone = weight_alone * share
+                r.class_probs[2 * it + b] = weights
+                r.self_prob[2 * it + b] = jnp.broadcast_to(weight_alone, (HEADS8, 128))
+                span = first[:, b * patches : (b + 1) * patches]
+                spread_out.append((2 * it + b, weights, weight_alone, span))
+        for image, weights, weight_alone, span in spread_out:
+            mixed = nt(weights.astype(BF16), span)
+            r.mixed[image] = mixed + weight_alone * r.class_first[image]
         return carry
 
-    lax.fori_loop(0, pairs // 2, class_forward, 0, unroll=2)
+    lax.fori_loop(0, pairs // 2, class_forward, 0)
     if inside:
         pl.semaphore_wait(barrier, 2 * n_img - 1)
         to_peers(r.w_own.at[seg], r.w_all.at[seg, me], r.l_weights)
         to_peers(r.s_own.at[seg], r.s_all.at[seg, me], r.l_shrink)
-    lax.fori_loop(pairs // 2, pairs, class_forward, 0, unroll=2)
 
     mixed = r.mixed[...].reshape(rows * HEADS8, width).astype(BF16)
     class_context = gather_heads(nn(mixed, r.frozen_triple[:, 2 * width :])).astype(BF16)
@@ -639,14 +650,22 @@
     stages = [loads[a:b] for a, b in zip(bounds, bounds[1:])]
     stages[0] = firsts[early:] + [tok_in] + stages[0]
     stages[1] = [cot_in] + stages[1]
-    for stage in stages + [firsts[:early] + earlier + [rows_in]]:
-        for load in stage:
-            load.start()
+    stages[3] = stages[3] + [rows_in] + firsts[:early] + earlier
+
+    def ask(*wanted):
+        for stage in wanted:
+            for load in stages[stage]:
+                load.start()
 
     def ready(stage):
         for load in stages[stage]:
             load.wait()
-
+        if stage == 0:
+            ask(1, 2)
+        if stage == 1:
+            ask(3)
+
+    ask(0)
     ready(0)
     gain_row = r.frozen_gain[...].astype(F32).reshape(1, width)
     regain_row = r.frozen_regain[...].astype(F32).reshape(1, width)
@@ -663,6 +682,7 @@
         wait = ready if it == early else lambda stage: None
         patch_pair(r, dims, it, it - early, following, wait)
     ready(3)
+    rows_out.start()
     out = pltpu.make_async_copy(r.tok, r.patch_output.at[last], r.late_sem.at[3])
     out.start()
 
@@ -679,38 +699,40 @@
     total = jnp.sum(spread(low * r.class_context[...]), axis=1, keepdims=True)
     r.class_total[...] = jnp.broadcast_to(total, (rows * HEADS8, 128)).reshape(rows, HEADS8, 128)
     r.ungainT[...] = 1.0 / r.gainT[:, 0:patches]
-    for load in firsts[:early] + earlier + [rows_in]:
-        load.wait()
-    rows_out.start()
-
-    def correct(it, carry):
-        first = r.firstT[it]
-        inverse = r.stat[it, 1:2, :]
-        left, right, along = [], [], []
-        maps = jnp.concatenate([r.low_map[2 * it + b] for b in range(2)], axis=0)
-        probs_grads = nn(maps.astype(BF16), first)
-        for b in range(2):
-            image = 2 * it + b
-            span = slice(b * patches, (b + 1) * patches)
-            part = probs_grads[b * HEADS8 : (b + 1) * HEADS8, span]
-            weights = r.class_probs[image]
-            score_grad = weights * (part - r.class_total[image][:, 0:1])
-            r.mixed[image] = nt(score_grad.astype(BF16), first[:, span])
-            toward = jnp.concatenate([r.query_map[image], r.low_map[image]], axis=0) * gain_row
-            left.append((toward - mean(toward, 1)).astype(BF16))
-            scaled = jnp.concatenate([score_grad * LN2, weights], axis=0) * inverse[:, span]
-            right.append(scaled.astype(BF16))
-            scores = jnp.concatenate([r.class_scores[image], part], axis=0)
-            along.append(jnp.sum(scaled * scores, axis=0, keepdims=True) * (1.0 / width))
-        for b in range(2):
-            span = slice(b * patches, (b + 1) * patches)
-            back = tn(left[b], right[b]) - first[:, span].astype(F32) * (r.ungainT[...] * along[b])
+
+    def correct(step, carry):
+        turns = [2 * step, 2 * step + 1]
+        grads = []
+        for it in turns:
+            maps = jnp.concatenate([r.low_map[2 * it + b] for b in range(2)], axis=0)
+            grads.append(nn(maps.astype(BF16), r.firstT[it]))
+        small = []
+        for it, grad in zip(turns, grads):
+            for b in range(2):
+                image = 2 * it + b
+                span = slice(b * patches, (b + 1) * patches)
+                part = grad[b * HEADS8 : (b + 1) * HEADS8, span]
+                weights = r.class_probs[image]
+                score_grad = weights * (part - r.class_total[image][:, 0:1])
+                toward = jnp.concatenate([r.query_map[image], r.low_map[image]], axis=0) * gain_row
+                left = (toward - mean(toward, 1)).astype(BF16)
+                right = jnp.concatenate([score_grad * LN2, weights], axis=0)
+                right = right * r.stat[it, 1:2, span]
+                scores = jnp.concatenate([r.class_scores[image], part], axis=0)
+                along = jnp.sum(right * scores, axis=0, keepdims=True) * (1.0 / width)
+                small.append((it, image, span, score_grad, left, right.astype(BF16), along))
+        products = [tn(left, right) for _, _, _, _, left, right, _ in small]
+        for product, (it, image, span, score_grad, _, _, along) in zip(products, small):
+            first = r.firstT[it, :, span]
+            r.mixed[image] = nt(score_grad.astype(BF16), first)
+            back = product - first.astype(F32) * (r.ungainT[...] * along)
             result = r.input_grad[it, :, span].astype(F32) + back
-            r.result[2 * it + b] = result.astype(BF16).T
-        pair_copy(r.result, r.patch_gradient, r.back_sem, it).start()
+            r.result[image] = result.astype(BF16).T
+        for it in turns:
+            pair_copy(r.result, r.patch_gradient, r.back_sem, it).start()
         return carry
 
-    lax.fori_loop(0, pairs, correct, 0, unroll=2)
+    lax.fori_loop(0, pairs // 2, correct, 0)
 
     self_prob = r.self_prob[...].reshape(rows * HEADS8, 128)[:, 0:1]
     tall_q = spread(packed[:, 0:width])

time: 110 us -> 105 us (0.955)
  Pallas kernels: 109 us -> 103 us
    pallas_call x1, Pallas kernels: 87.2 us -> 84.5 us  [local(): pl.pallas_call(functools.partial(patch_kernel, SimpleNamespace(names=name...]
    pallas_call x1, Pallas kernels: 21.4 us -> 19 us  [local(): pl.pallas_call(functools.partial(finish_kernel, SimpleNamespace(**sizes))...]
where the time goes in v4:
time: 105 us; the launch traced here: 104 us
  Pallas kernels  103 us (98%)
    pallas_call x1, Pallas kernels, local(): pl.pallas_call(functools.partial(patch_kernel, SimpleNamespace(names=name...  84.5 us
    pallas_call x1, Pallas kernels, local(): pl.pallas_call(functools.partial(finish_kernel, SimpleNamespace(**sizes))...  19 us

profile of v4, /device:TPU:0, one launch (start us, length us, event | category | flops | bytes accessed | tf_op | source)
XLA Modules:
  0.0 104.3 jit_solution(13426391438799215312)
XLA Ops:
  0.6 84.5 %shard_map.240 = (bf16[16,256,384]{2,1,0:T(8,128)(2,1)}, bf16[8,384,512]{2,1,0:T(8,128)(2,1)}, bf16[8,384,512]{2,1,0:T(8,128)(2,1)}, bf16[1152,384]{1,0:T(8,128)...) custom-call(bf16[16,256,384]{2,1,0:T(8,128)(2,1)} %bitcast.10, ...), custom_call_target="tpu_custom_call" | custom-call | tf_op jit(solution)/shard_map/pallas_call | solution.py:1146
  85.1 19.0 %shard_map.241 = (bf16[16,256,384]{2,1,0:T(8,128)(2,1)}, bf16[16,256,384]{2,1,0:T(8,128)(2,1)}, bf16[16,384]{1,0:T(8,128)(2,1)}, bf16[16,384]{1,0:T(8,128)(2,1)}...) custom-call(bf16[16,256,384]{2,1,0:T(8,128)(2,1)} %bitcast.11, ...), custom_call_target="tpu_custom_call" | custom-call | tf_op jit(solution)/shard_map/pallas_call | solution.py:1228

commit v5 on v4

--- a/solution.py
+++ b/solution.py
@@ -169,7 +169,8 @@
     merged = nn(r.mergeT[...], ctx[...])
     upstream = jnp.concatenate([r.cot[2 * slot + b].T for b in range(2)], axis=1)
     half_upstream = upstream * BF16(0.5)
-    chunks = [slice(c, c + width) for c in range(0, hidden, width)]
+    third = hidden // 3
+    chunks = [slice(c, c + third) for c in range(0, hidden, third)]
 
     def active_grad(at):
         return nn(r.frozen_shrink[at, :], half_upstream).astype(BF16)

time: 105 us -> 104 us (level)
    pallas_call x1, Pallas kernels: 84.5 us -> 82.7 us  [local(): pl.pallas_call(functools.partial(patch_kernel, SimpleNamespace(names=name...]
where the time goes in v5:
time: 104 us; the launch traced here: 102 us
  Pallas kernels  102 us (98%)
    pallas_call x1, Pallas kernels, local(): pl.pallas_call(functools.partial(patch_kernel, SimpleNamespace(names=name...  82.7 us
    pallas_call x1, Pallas kernels, local(): pl.pallas_call(functools.partial(finish_kernel, SimpleNamespace(**sizes))...  18.9 us

profile of v5, /device:TPU:0, one launch (start us, length us, event | category | flops | bytes accessed | tf_op | source)
XLA Modules:
  0.0 102.4 jit_solution(9132952350642366056)
XLA Ops:
  0.6 82.7 %shard_map.240 = (bf16[16,256,384]{2,1,0:T(8,128)(2,1)}, bf16[8,384,512]{2,1,0:T(8,128)(2,1)}, bf16[8,384,512]{2,1,0:T(8,128)(2,1)}, bf16[1152,384]{1,0:T(8,128)...) custom-call(bf16[16,256,384]{2,1,0:T(8,128)(2,1)} %bitcast.10, ...), custom_call_target="tpu_custom_call" | custom-call | tf_op jit(solution)/shard_map/pallas_call | solution.py:1147
  83.3 18.9 %shard_map.241 = (bf16[16,256,384]{2,1,0:T(8,128)(2,1)}, bf16[16,256,384]{2,1,0:T(8,128)(2,1)}, bf16[16,384]{1,0:T(8,128)(2,1)}, bf16[16,384]{1,0:T(8,128)(2,1)}...) custom-call(bf16[16,256,384]{2,1,0:T(8,128)(2,1)} %bitcast.11, ...), custom_call_target="tpu_custom_call" | custom-call | tf_op jit(solution)/shard_map/pallas_call | solution.py:1229

commit v6 on v5

--- a/solution.py
+++ b/solution.py
@@ -399,7 +399,7 @@
         return first
 
     def class_forward(step, carry):
-        turns = [2 * step, 2 * step + 1]
+        turns = [4 * step + k for k in range(4)]
         firsts = [class_norm(it) for it in turns]
         scores = []
         for it, first in zip(turns, firsts):
@@ -426,7 +426,7 @@
             r.mixed[image] = mixed + weight_alone * r.class_first[image]
         return carry
 
-    lax.fori_loop(0, pairs // 2, class_forward, 0)
+    lax.fori_loop(0, pairs // 4, class_forward, 0)
     if inside:
         pl.semaphore_wait(barrier, 2 * n_img - 1)
         to_peers(r.w_own.at[seg], r.w_all.at[seg, me], r.l_weights)
@@ -702,7 +702,7 @@
     r.ungainT[...] = 1.0 / r.gainT[:, 0:patches]
 
     def correct(step, carry):
-        turns = [2 * step, 2 * step + 1]
+        turns = [4 * step + k for k in range(4)]
         grads = []
         for it in turns:
             maps = jnp.concatenate([r.low_map[2 * it + b] for b in range(2)], axis=0)
@@ -733,7 +733,7 @@
             pair_copy(r.result, r.patch_gradient, r.back_sem, it).start()
         return carry
 
-    lax.fori_loop(0, pairs // 2, correct, 0)
+    lax.fori_loop(0, pairs // 4, correct, 0)
 
     self_prob = r.self_prob[...].reshape(rows * HEADS8, 128)[:, 0:1]
     tall_q = spread(packed[:, 0:width])

time: 104 us -> 103 us (level)
  no operation moved by 1% of the time
where the time goes in v6:
time: 103 us; the launch traced here: 102 us
  Pallas kernels  101 us (98%)
    pallas_call x1, Pallas kernels, local(): pl.pallas_call(functools.partial(patch_kernel, SimpleNamespace(names=name...  82.2 us
    pallas_call x1, Pallas kernels, local(): pl.pallas_call(functools.partial(finish_kernel, SimpleNamespace(**sizes))...  18.9 us

profile of v6, /device:TPU:0, one launch (start us, length us, event | category | flops | bytes accessed | tf_op | source)
XLA Modules:
  0.0 101.9 jit_solution(10285056689371326003)
XLA Ops:
  0.6 82.2 %shard_map.240 = (bf16[16,256,384]{2,1,0:T(8,128)(2,1)}, bf16[8,384,512]{2,1,0:T(8,128)(2,1)}, bf16[8,384,512]{2,1,0:T(8,128)(2,1)}, bf16[1152,384]{1,0:T(8,128)...) custom-call(bf16[16,256,384]{2,1,0:T(8,128)(2,1)} %bitcast.10, ...), custom_call_target="tpu_custom_call" | custom-call | tf_op jit(solution)/shard_map/pallas_call | solution.py:1147
  82.9 18.9 %shard_map.241 = (bf16[16,256,384]{2,1,0:T(8,128)(2,1)}, bf16[16,256,384]{2,1,0:T(8,128)(2,1)}, bf16[16,384]{1,0:T(8,128)(2,1)}, bf16[16,384]{1,0:T(8,128)(2,1)}...) custom-call(bf16[16,256,384]{2,1,0:T(8,128)(2,1)} %bitcast.11, ...), custom_call_target="tpu_custom_call" | custom-call | tf_op jit(solution)/shard_map/pallas_call | solution.py:1229
